TPU v7x, 1024 devices: a whole 4x4x32 slice. The times are simulated.
1024 devices in a mesh: rows: 256 (over z, x, core), cols: 4 (over y).
Axes of the slice: x: 4, y: 4, z: 32, core: 2. Of those that a mesh axis runs over, the one named last changes fastest.
Arguments:
- a_vals: bfloat16 [8192, 64, 512], P(('rows', 'cols')), may hold values from -0.25 to 0.25
- a_cols: int32 [8192, 8], P('rows'), may hold values from 0 to 8191, as said below
- p_vals: bfloat16 [8192, 64, 256], P('rows'), may hold values from -1.5 to 1.5
- p_cols: int32 [8192, 4], replicated, may hold values from 0 to 1023, as said below
- colpos: int32 [1024], replicated, may hold values from 0 to 3, as said below
Outputs:
- coarse_matrix: float32 [1024, 64, 768], P('rows', None, 'cols')
Inputs may be any that keep to these rules, and one draw needn't show every extreme that they name: a_cols[i, 0] = i, and every entry j of row i satisfies |j - i| <= 4. `p_cols`: the 4 entries of a row are distinct. The first is the row's aggregate, in the row's partition; each coarse block is the first entry of exactly 8 rows. The others lie in the row's partition, or also in partition i // 32 - 1 when i % 32 < 4, or in partition i // 32 + 1 when i % 32 >= 28. `colpos`: over each partition's 4 coarse blocks, a permutation of 0 to 3.
All inputs are finite; a program needn't handle non-finite values.
Results may differ from a plain program's by a relative error of at most 0.0029.
Values may be sent and summed in bfloat16 or wider, within the bound.
No kernel may reach another device: no remote copies, remote signals or barrier semaphores. Data moves between devices by JAX's collectives and lax.ppermute only.
A program may use at most 64 MiB of HBM per device.

v0:
```python
import jax
import jax.numpy as jnp
from jax import lax
from jax.sharding import PartitionSpec as P

KA = 8
KP = 4
HB = 4
CBC = 1


def extended_2(block, sides, width):
    for axis, dim in sides:
        count = lax.axis_size(axis)
        forward = [(i, i + 1) for i in range(count - 1)]
        backward = [(target, source) for source, target in forward]
        low = lax.ppermute(
            lax.slice_in_dim(block, block.shape[dim] - width, None, axis=dim), axis, forward
        )
        high = lax.ppermute(lax.slice_in_dim(block, 0, width, axis=dim), axis, backward)
        block = jnp.concatenate([low, block, high], axis=dim)
    return block


def window_slots(ext_cols, win_pos, part_idx, coarse):
    relative = ext_cols - (part_idx - 1) * coarse
    matches = relative[:, :, None] == jnp.arange(3 * coarse, dtype=jnp.int32)[None, None, :]
    col_slot = jnp.sum(jnp.where(matches, win_pos[None, None, :], 0), axis=2)
    is_valid = jnp.any(matches, axis=2)
    owner_group = col_slot // CBC
    inner_slot = relative // coarse * CBC + col_slot % CBC
    return (relative, is_valid, owner_group, inner_slot)


def dense_window(ext_p, slots, win_width):
    count_rows = ext_p.shape[0]
    block_size = ext_p.shape[1]
    picker = (slots[:, :, None] == jnp.arange(win_width, dtype=jnp.int32)[None, None, :]).astype(
        jnp.bfloat16
    )
    shaped = ext_p.reshape(count_rows, block_size, KP, block_size)
    dense_p = jnp.einsum("jmw,jbme->jbwe", picker, shaped, preferred_element_type=jnp.float32)
    return dense_p.astype(jnp.bfloat16).reshape(count_rows, block_size, win_width * block_size)


def ap_block(a_piece, row_cols, dense_p, first_row):
    count_rows = a_piece.shape[0]
    block_size = a_piece.shape[1]
    local_idx = row_cols - first_row
    picked = jnp.take(dense_p, local_idx, axis=0)
    picked = picked.reshape(count_rows, KA * block_size, dense_p.shape[2])
    accum = lax.dot_general(
        a_piece, picked, (((2,), (1,)), ((0,), (0,))), preferred_element_type=jnp.float32
    )
    return accum.astype(jnp.bfloat16)


def coarse_terms(own_p, ap_rows, own_rel, coarse):
    block_size = own_p.shape[1]
    win_width = 3 * coarse
    spread_p = dense_window(own_p, own_rel, win_width)
    summed = lax.dot_general(
        spread_p, ap_rows, (((0, 1), (0, 1)), ((), ())), preferred_element_type=jnp.float32
    )
    return summed.reshape(win_width, block_size, ap_rows.shape[2])


def on_device(a_vals, a_cols, p_vals, p_cols, colpos):
    num_groups = lax.axis_size("cols")
    my_group = lax.axis_index("cols")
    part_idx = lax.axis_index("rows")
    fine_rows = p_vals.shape[0]
    block_size = p_vals.shape[1]
    coarse = CBC * num_groups
    group_width = 3 * CBC
    padded_cols = jnp.pad(p_cols, ((HB, HB), (0, 0)))
    ext_cols = lax.dynamic_slice_in_dim(padded_cols, part_idx * fine_rows, fine_rows + 2 * HB, 0)
    padded_pos = jnp.pad(colpos, (coarse, coarse))
    win_pos = lax.dynamic_slice_in_dim(padded_pos, part_idx * coarse, 3 * coarse, 0)
    ext_p = extended_2(p_vals, (("rows", 0),), HB)
    relative, is_valid, owner_group, inner_slot = window_slots(ext_cols, win_pos, part_idx, coarse)
    first_fine = part_idx * fine_rows - HB
    own_count = a_vals.shape[0]
    own_start = my_group * own_count
    slots = jnp.where(is_valid, owner_group * group_width + inner_slot, -1)
    near_p = lax.dynamic_slice_in_dim(ext_p, own_start, own_count + 2 * HB, 0)
    near_slots = lax.dynamic_slice_in_dim(slots, own_start, own_count + 2 * HB, 0)
    dense_p = dense_window(near_p, near_slots, num_groups * group_width)
    row_cols = lax.dynamic_slice_in_dim(a_cols, own_start, own_count, 0)
    ap_rows = ap_block(a_vals, row_cols, dense_p, first_fine + own_start)
    own_p = lax.dynamic_slice_in_dim(p_vals, own_start, own_count, 0)
    own_rel = lax.dynamic_slice_in_dim(relative, HB + own_start, own_count, 0)
    all_terms = coarse_terms(own_p, ap_rows, own_rel, coarse)
    part_terms = lax.psum_scatter(all_terms, "cols", scatter_dimension=2, tiled=True)
    band_width = CBC * block_size
    extended = extended_2(part_terms, (("rows", 0),), coarse)
    from_left = extended[:coarse, :, band_width:]
    from_right = extended[4 * coarse :, :, : 2 * band_width]
    zero_cols = jnp.zeros((coarse, block_size, band_width), jnp.float32)
    middle = part_terms[coarse : 2 * coarse]
    summed = (
        middle
        + jnp.concatenate([from_left, zero_cols], axis=2)
        + jnp.concatenate([zero_cols, from_right], axis=2)
    )
    return summed


def solution(mesh):
    placed = (P(("rows", "cols"), None, None), P("rows", None), P("rows", None, None), P(), P())
    return jax.shard_map(
        on_device, mesh=mesh, in_specs=placed, out_specs=P("rows", None, "cols"), check_vma=False
    )
```

profile of v0, /device:TPU:103, one launch (start us, length us, event | category | flops | bytes accessed | tf_op | source)
XLA Modules:
  0.0 142.3 jit_solution(360880678133318459)
XLA Ops:
  6.5 1.7 %fusion.17 = (bf16[4,64,256]{2,1,0:T(8,128)(2,1)S(1)}, bf16[4,64,256]{2,1,0:T(8,128)(2,1)}) fusion(bf16[32,64,256]{2,1,0:T(8,128)(2,1)} %param.7), kind=kLoop, calls=%fused_computation.42 | loop fusion | bytes 524288 | tf_op jit(solution)/shard_map/slice | solution.py:20
  8.2 5.2 %collective-permute-start = (bf16[4,64,256]{2,1,0:T(8,128)(2,1)}, bf16[4,64,256]{2,1,0:T(8,128)(2,1)}, u32[]{:S(2)}, u32[]{:S(2)}) collective-permute-start(bf16[4,64,256]{2,1,0:T(8,128)(2,1)} %get-tuple-element.11), channel_id=1, source_target_pairs={{0,4},{4,8},{8,12},{12,16},{16,20},{20,24},{24,28},{28,32},{32,36}... | collective-permute-start | bytes 393224 | tf_op jit(solution)/shard_map/ppermute | solution.py:17
  13.5 1.9 %collective-permute-start.1 = (bf16[4,64,256]{2,1,0:T(8,128)(2,1)S(1)}, bf16[4,64,256]{2,1,0:T(8,128)(2,1)}, u32[]{:S(2)}, u32[]{:S(2)}) collective-permute-start(bf16[4,64,256]{2,1,0:T(8,128)(2,1)S(1)} %get-tuple-element.10), channel_id=1, source_target_pairs={{4,0},{8,4},{12,8},{16,12},{20,16},{24,20},{28,24},{32,28},{36,32}... | collective-permute-start | bytes 393224 | tf_op jit(solution)/shard_map/ppermute | solution.py:20
  15.4 0.8 fusion.14
  17.2 1.0 constant_dynamic-slice_fusion.2
  18.5 0.8 fusion.13
  20.0 0.8 convert_bitcast_fusion.1
  21.4 1.3 reshape.27
  22.7 2.2 %dot_general.18 = bf16[12,64,8,64]{1,0,3,2:T(8,128)(2,1)} reshape(bf16[768,8,64]{0,2,1:T(8,128)(2,1)S(1)} %bitcast.38) | data formatting | bytes 1572864 | tf_op jit(solution)/shard_map/dot_general | solution.py:62
  25.0 1.1 fusion.3
  26.5 3.3 %convert_bitcast_fusion = bf16[16,64,12,64]{3,2,1,0:T(8,128)(2,1)} fusion(bf16[16,64,4,64]{3,2,1,0:T(4,128)(2,1)S(1)} %reshape.28, s32[16,4]{1,0:T(8,128)S(1)} %copy.25), kind=kOutput, calls=%fused_computation.2 | convolution fusion | flops 7078656 | bytes 2097408 | tf_op jit(solution)/shard_map/jmw,jbme->jbwe/dot_general | solution.py:42
  29.8 5.2 %reshape.29 = bf16[16,64,768]{2,1,0:T(8,128)(2,1)S(1)} reshape(bf16[16,64,12,64]{3,2,1,0:T(8,128)(2,1)} %convert_bitcast_fusion) | data formatting | bytes 3145728 | tf_op jit(solution)/shard_map/reshape | solution.py:43
  35.0 3.6 %gather_fusion = bf16[64,64,768]{2,1,0:T(8,128)(2,1)} fusion(bf16[16,64,768]{2,1,0:T(8,128)(2,1)S(1)} %reshape.29, s32[1024]{0:T(1024)S(1)} %pad_clamp_fusion), kind=kCustom, calls=%fused_computation | custom fusion | bytes 12583168 | tf_op jit(solution)/shard_map/jit(_take)/gather | solution.py:50
  38.6 6.7 %bitcast_select_fusion = bf16[8,512,768]{2,1,0:T(8,128)(2,1)} fusion(pred[8,512]{1,0:T(8,128)(4,1)S(1)} %broadcast_in_dim.39, bf16[8,512,768]{2,1,0:T(8,128)(2,1)} %bitcast.35), kind=kLoop, calls=%fused_computation.1 | loop fusion | flops 3145728 | bytes 12587008 | tf_op jit(solution)/shard_map/jit(_take)/select_n | solution.py:50
  45.3 5.4 %convolution_bitcast_fusion = f32[12,64,768]{2,1,0:T(8,128)S(1)} fusion(bf16[12,64,8,64]{1,0,3,2:T(8,128)(2,1)} %dot_general.18, bf16[8,64,512]{2,1,0:T(8,128)(2,1)S(1)} %copy-done, bf16[8,512,768]{2,1,0:T(8,128)(2,1)} %bitcast_select_fusion), kind=kOutput, calls=%fused_computation.4 | convolution fusion | flops 1007026176 | bytes 9961472 | tf_op jit(solution)/shard_map/dot_general | solution.py:62
  50.7 5.1 %copy.31 = f32[12,64,768]{1,0,2:T(8,128)} copy(f32[12,64,768]{2,1,0:T(8,128)S(1)} %convolution_bitcast_fusion) | data formatting | bytes 4718592
  55.8 5.5 %reshape.45 = f32[768,768]{1,0:T(8,128)} reshape(f32[768,12,64]{2,1,0:T(8,128)} %bitcast.36) | data formatting | bytes 4718592
  61.3 55.4 %reduce-scatter.4.cloned.1.call-done = f32[192,768]{1,0:T(8,128)} async-done(((f32[768,768]{1,0:T(8,128)}), f32[192,768]{1,0:T(8,128)}) %reduce-scatter.4.cloned.1.call-update) | async-done | bytes 589840
  116.7 1.4 reshape.46
  118.5 4.9 %collective-permute-start.2 = (f32[4,64,192]{2,1,0:T(8,128)S(1)}, f32[4,64,192]{2,1,0:T(8,128)S(1)}, u32[]{:S(2)}, u32[]{:S(2)}) collective-permute-start(f32[4,64,192]{2,1,0:T(8,128)S(1)} %copy.34), channel_id=1, source_target_pairs={{0,4},{4,8},{8,12},{12,16},{16,20},{20,24},{24,28},{28,32},{32,36}... | collective-permute-start | bytes 589832 | tf_op jit(solution)/shard_map/ppermute | solution.py:17
  123.6 1.9 %collective-permute-start.3 = (f32[4,64,192]{2,1,0:T(8,128)S(1)}, f32[4,64,192]{2,1,0:T(8,128)S(1)}, u32[]{:S(2)}, u32[]{:S(2)}) collective-permute-start(f32[4,64,192]{2,1,0:T(8,128)S(1)} %copy.35), channel_id=1, source_target_pairs={{4,0},{8,4},{12,8},{16,12},{20,16},{24,20},{28,24},{32,28},{36,32}... | collective-permute-start | bytes 589832 | tf_op jit(solution)/shard_map/ppermute | solution.py:20
  125.7 1.0 collective-permute-done.2
  126.7 7.8 %collective-permute-done.3 = f32[4,64,192]{2,1,0:T(8,128)S(1)} collective-permute-done((f32[4,64,192]{2,1,0:T(8,128)S(1)}, f32[4,64,192]{2,1,0:T(8,128)S(1)}, u32[]{:S(2)}, u32[]{:S(2)}) %collective-permute-start.3) | collective-permute-done | bytes 196640 | tf_op jit(solution)/shard_map/ppermute | solution.py:20
  134.6 0.8 pad_add_fusion
  (30 shorter events, 3.9 us)
Async XLA Ops:
  6.5 38.8 %copy-start = (bf16[8,64,512]{2,1,0:T(8,128)(2,1)S(1)}, bf16[8,64,512]{2,1,0:T(8,128)(2,1)}, u32[]{:S(2)}) copy-start(bf16[8,64,512]{2,1,0:T(8,128)(2,1)} %param.5) | copy-start | bytes 1572868
  6.5 110.1 %reduce-scatter.4.cloned.1.call-start = ((), (), s32[]{:S(2)}) async-start(), calls=%async_computation.1 | async-start | bytes 2949120
  8.2 16.7 %collective-permute-start = (bf16[4,64,256]{2,1,0:T(8,128)(2,1)}, bf16[4,64,256]{2,1,0:T(8,128)(2,1)}, u32[]{:S(2)}, u32[]{:S(2)}) collective-permute-start(bf16[4,64,256]{2,1,0:T(8,128)(2,1)} %get-tuple-element.11), channel_id=1, source_target_pairs={{0,4},{4,8},{8,12},{12,16},{16,20},{20,24},{24,28},{28,32},{32,36}... | collective-permute-start | bytes 393224 | tf_op jit(solution)/shard_map/ppermute | solution.py:17
  13.5 11.5 %collective-permute-start.1 = (bf16[4,64,256]{2,1,0:T(8,128)(2,1)S(1)}, bf16[4,64,256]{2,1,0:T(8,128)(2,1)}, u32[]{:S(2)}, u32[]{:S(2)}) collective-permute-start(bf16[4,64,256]{2,1,0:T(8,128)(2,1)S(1)} %get-tuple-element.10), channel_id=1, source_target_pairs={{4,0},{8,4},{12,8},{16,12},{20,16},{24,20},{28,24},{32,28},{36,32}... | collective-permute-start | bytes 393224 | tf_op jit(solution)/shard_map/ppermute | solution.py:20
  22.7 2.3 %copy-start.1 = (bf16[32,64,256]{2,1,0:T(8,128)(2,1)S(1)}, bf16[32,64,256]{2,1,0:T(8,128)(2,1)}, u32[]{:S(2)}) copy-start(bf16[32,64,256]{2,1,0:T(8,128)(2,1)} %param.7) | copy-start | bytes 3145732
  118.5 8.2 %collective-permute-start.2 = (f32[4,64,192]{2,1,0:T(8,128)S(1)}, f32[4,64,192]{2,1,0:T(8,128)S(1)}, u32[]{:S(2)}, u32[]{:S(2)}) collective-permute-start(f32[4,64,192]{2,1,0:T(8,128)S(1)} %copy.34), channel_id=1, source_target_pairs={{0,4},{4,8},{8,12},{12,16},{16,20},{20,24},{24,28},{28,32},{32,36}... | collective-permute-start | bytes 589832 | tf_op jit(solution)/shard_map/ppermute | solution.py:17
  123.6 11.0 %collective-permute-start.3 = (f32[4,64,192]{2,1,0:T(8,128)S(1)}, f32[4,64,192]{2,1,0:T(8,128)S(1)}, u32[]{:S(2)}, u32[]{:S(2)}) collective-permute-start(f32[4,64,192]{2,1,0:T(8,128)S(1)} %copy.35), channel_id=1, source_target_pairs={{4,0},{8,4},{12,8},{16,12},{20,16},{24,20},{28,24},{32,28},{36,32}... | collective-permute-start | bytes 589832 | tf_op jit(solution)/shard_map/ppermute | solution.py:20
Sparse Core Ops, SparseCore 0:
  61.4 55.2 reduce-scatter.3
where the time goes:
time: 143 us; the launch traced here: 142 us
  waiting for transfers between devices  64.2 us (45%)
  local copies, waits for them, and re-layouts  29.9 us (21%)
  starting transfers between devices  13.9 us (10%)
  between operations  13.6 us (10%)
  other arithmetic  11.1 us (8%)
  matrix products  9.5 us (7%)
    unnamed x2, waiting for transfers between devices  55.4 us
    unnamed x10, local copies, waits for them, and re-layouts  12.5 us
    ppermute x2, starting transfers between devices, extended_2(): lax.ppermute(lax.slice_in_dim(block, block.shape[dim] - width, None, axis...  10.1 us
    ppermute x2, waiting for transfers between devices, extended_2(): lax.ppermute(lax.slice_in_dim(block, 0, width, axis=dim), axis, backward)  7.82 us
    select_n x1, other arithmetic, ap_block(): picked = jnp.take(dense_p, local_idx, axis=0)  6.7 us
    reshape x2, local copies, waits for them, and re-layouts, dense_window(): dense_p.astype(jnp.bfloat16)  6.48 us
    dot_general x1, matrix products, coarse_terms(): lax.dot_general(spread_p, ap_rows, (((0, 1), (0, 1)), ((), ())), preferre...  5.37 us
    dot_general x2, matrix products, dense_window(): jnp.einsum('jmw,jbme->jbwe', picker, shaped, preferred_element_type=jnp.f...  4.13 us
  transfers between devices with their start and end apart: 5, of which 3 were waited for; matrix products, arithmetic and copies ran while one was open for 7% of the time, Pallas kernels for 0%

commit v1 on v0

v1 whole, which is shorter than its diff:
```python
import jax
import jax.numpy as jnp
from jax import lax
from jax.experimental import pallas as pl
from jax.experimental.pallas import tpu as pltpu
from jax.sharding import PartitionSpec as P

B = 64
KA = 8
KP = 4
HB = 4
LANES = 2 * B
VMEM = pl.BlockSpec(memory_space=pltpu.VMEM)
SMEM = pl.BlockSpec(memory_space=pltpu.SMEM)


def spread_row(x, slot_ref, base, groups, left):
    x = x.astype(jnp.float32)
    pieces = []
    for v in range(KP // 2):
        pair = x[:, v * LANES : (v + 1) * LANES]
        turned = pltpu.roll(pair, B, 1)
        pieces.append((pair, turned, slot_ref[base + 2 * v], slot_ref[base + 2 * v + 1]))
    out = []
    for c in range(groups):
        total = None
        for pair, turned, s0, s1 in pieces:
            def flag(s, w):
                return (s == w).astype(jnp.float32)
            keep = jnp.where(left, flag(s0, 2 * c), flag(s1, 2 * c + 1))
            swap = jnp.where(left, flag(s1, 2 * c), flag(s0, 2 * c + 1))
            term = pair * keep + turned * swap
            total = term if total is None else total + term
        out.append(total.astype(jnp.bfloat16))
    return out


def terms_kernel(slot_ref, idx_ref, g_ref, a_ref, p_ref, halo_ref, own_ref, edge_ref, pd_ref, ap_ref):
    groups = own_ref.shape[0]
    count = a_ref.shape[0]
    fine = p_ref.shape[0]
    g = g_ref[0]
    lower = g < groups // 2
    left = lax.broadcasted_iota(jnp.int32, (1, LANES), 1) < B
    for j in range(count + 2 * HB):
        row = jnp.clip(count * g - HB + j, 0, fine - 1)
        x = p_ref[row]
        if j < HB:
            x = jnp.where(g == 0, halo_ref[j], x)
        if j >= count + HB:
            x = jnp.where(g == groups - 1, halo_ref[j - count - HB], x)
        for c, block in enumerate(spread_row(x, slot_ref, j * KP, groups, left)):
            pd_ref[j * B : (j + 1) * B, c * LANES : (c + 1) * LANES] = block
    for i in range(count):
        picked = jnp.concatenate(
            [pd_ref[pl.ds(pl.multiple_of(idx_ref[i * KA + k] * B, B), B), :] for k in range(KA)], axis=0
        )
        ap = jnp.dot(a_ref[i], picked, preferred_element_type=jnp.float32)
        ap_ref[i * B : (i + 1) * B, :] = ap.astype(jnp.bfloat16)
    own_p = pd_ref[HB * B : (HB + count) * B, :]
    terms = lax.dot_general(
        own_p, ap_ref[...], (((0,), (0,)), ((), ())), preferred_element_type=jnp.float32
    )
    for row in range(groups):
        first = terms[2 * row * B : (2 * row + 1) * B]
        second = terms[(2 * row + 1) * B : (2 * row + 2) * B]
        own = jnp.where(lower, second, first)
        edge = jnp.where(lower, first, second).astype(jnp.bfloat16)
        for c in range(groups):
            own_ref[c, row * B : (row + 1) * B, :] = own[:, c * LANES : (c + 1) * LANES]
            edge_ref[c, row * B : (row + 1) * B, :] = edge[:, c * LANES : (c + 1) * LANES]


def final_kernel(pos_ref, got_ref, out_ref, low_ref, high_ref):
    groups = got_ref.shape[0]
    half = groups // 2
    low = got_ref[0].astype(jnp.float32)
    high = got_ref[half].astype(jnp.float32)
    for g in range(1, half):
        low += got_ref[g].astype(jnp.float32)
        high += got_ref[half + g].astype(jnp.float32)
    low_ref[...] = low
    high_ref[...] = high
    left = lax.broadcasted_iota(jnp.int32, (1, LANES), 1) < B
    for h in range(out_ref.shape[0]):
        rows = pl.ds(pl.multiple_of(pos_ref[h] * B, B), B)
        high = high_ref[rows, :]
        out_ref[h, :, :LANES] = low_ref[rows, :] + jnp.where(left, 0.0, pltpu.roll(high, B, 1))
        out_ref[h, :, LANES:] = high[:, B:]


def on_device(a_vals, a_cols, p_vals, p_cols, colpos):
    groups = lax.axis_size("cols")
    parts = lax.axis_size("rows")
    g = lax.axis_index("cols")
    p = lax.axis_index("rows")
    count = a_vals.shape[0]
    fine = p_vals.shape[0]
    coarse = groups
    near = count + 2 * HB
    last = groups - 1

    edge_p = lax.dynamic_slice_in_dim(p_vals, jnp.where(g == 0, fine - HB, 0), HB, 0)
    inward = [(q * groups, (q + 1) * groups) for q in range(parts - 1)]
    inward += [((q + 1) * groups + last, q * groups + last) for q in range(parts - 1)]
    halo_p = lax.ppermute(edge_p, ("rows", "cols"), inward)

    start = p * fine + g * count
    near_cols = lax.dynamic_slice_in_dim(jnp.pad(p_cols, ((HB, HB), (0, 0))), start, near, 0)
    win_pos = lax.dynamic_slice_in_dim(jnp.pad(colpos, (coarse, coarse)), p * coarse, 3 * coarse, 0)
    relative = near_cols - (p - 1) * coarse
    match = relative[:, :, None] == jnp.arange(3 * coarse, dtype=jnp.int32)
    place = 2 * win_pos + jnp.arange(3 * coarse, dtype=jnp.int32) // coarse
    first_band = jnp.where(g < groups // 2, 0, 1)
    slots = jnp.sum(jnp.where(match, place - first_band, 0), axis=2).reshape(-1)
    own_cols = lax.dynamic_slice_in_dim(a_cols, g * count, count, 0)
    local = (own_cols - (start - HB)).reshape(-1)

    shape = (groups, coarse * B, LANES)
    own, edge = pl.pallas_call(
        terms_kernel,
        out_shape=(
            jax.ShapeDtypeStruct(shape, jnp.float32),
            jax.ShapeDtypeStruct(shape, jnp.bfloat16),
        ),
        in_specs=[SMEM, SMEM, SMEM, VMEM, VMEM, VMEM],
        out_specs=(VMEM, VMEM),
        scratch_shapes=[
            pltpu.VMEM((near * B, groups * LANES), jnp.bfloat16),
            pltpu.VMEM((count * B, groups * LANES), jnp.bfloat16),
        ],
        compiler_params=pltpu.CompilerParams(vmem_limit_bytes=32 << 20),
        name="terms",
    )(slots, local, jnp.reshape(g, (1,)), a_vals, p_vals, halo_p)

    across = [(q * groups, (q - 1) * groups + last) for q in range(1, parts)]
    across += [(target, source) for source, target in across]
    taken = lax.ppermute(edge, ("rows", "cols"), across)
    sent = (own + taken.astype(jnp.float32)).astype(jnp.bfloat16)
    got = lax.all_to_all(sent, "cols", 0, 0)

    return pl.pallas_call(
        final_kernel,
        out_shape=jax.ShapeDtypeStruct((coarse, B, 3 * B), jnp.float32),
        in_specs=[SMEM, VMEM],
        out_specs=VMEM,
        scratch_shapes=[pltpu.VMEM((coarse * B, LANES), jnp.float32)] * 2,
        name="final",
    )(win_pos[coarse : 2 * coarse], got)


def solution(mesh):
    placed = (P(("rows", "cols"), None, None), P("rows", None), P("rows", None, None), P(), P())
    return jax.shard_map(
        on_device, mesh=mesh, in_specs=placed, out_specs=P("rows", None, "cols"), check_vma=False
    )
```

time: 143 us -> 43.6 us (0.30)
  the two profiles are of different devices: /device:TPU:103 before, /device:TPU:1 now
where the time goes in v1:
time: 43.6 us; the launch traced here: 43.2 us
  waiting for transfers between devices  21.8 us (50%)
  starting transfers between devices  9.84 us (23%)
  local copies, waits for them, and re-layouts  6.12 us (14%)
  Pallas kernels  4.27 us (10%)
  other arithmetic  1.1 us (3%)
    ppermute x1, waiting for transfers between devices, on_device(): halo_p = lax.ppermute(edge_p, ('rows', 'cols'), inward)  9.85 us
    ppermute x1, waiting for transfers between devices, on_device(): taken = lax.ppermute(edge, ('rows', 'cols'), across)  6.97 us
    all_to_all x1, waiting for transfers between devices, on_device(): got = lax.all_to_all(sent, 'cols', 0, 0)  4.99 us
    ppermute x1, starting transfers between devices, on_device(): halo_p = lax.ppermute(edge_p, ('rows', 'cols'), inward)  4.51 us
    unnamed x12, local copies, waits for them, and re-layouts  4.18 us
    all_to_all x1, starting transfers between devices, on_device(): got = lax.all_to_all(sent, 'cols', 0, 0)  3.41 us
    pallas_call x1, Pallas kernels, on_device(): pl.pallas_call(terms_kernel, out_shape=(jax.ShapeDtypeStruct(shape, jnp.f...  2.48 us
    ppermute x1, starting transfers between devices, on_device(): taken = lax.ppermute(edge, ('rows', 'cols'), across)  1.92 us
  transfers between devices with their start and end apart: 3, of which 3 were waited for; matrix products, arithmetic and copies ran while one was open for 3% of the time, Pallas kernels for 0%

profile of v1, /device:TPU:1, one launch (start us, length us, event | category | flops | bytes accessed | tf_op | source)
XLA Modules:
  0.0 43.2 jit_solution(14665649768498353396)
XLA Ops:
  0.0 0.9 %constant_dynamic-slice_fusion = bf16[4,64,256]{2,1,0:T(8,128)(2,1)S(1)} fusion(bf16[32,64,256]{2,1,0:T(8,128)(2,1)} %p_ref.1, s32[]{:T(128)S(6)} %select_n.32), kind=kLoop, calls=%fused_computation.11 | loop fusion | bytes 262148 | tf_op jit(solution)/shard_map/dynamic_slice | solution.py:103
  1.0 4.5 %collective-permute-start = (bf16[4,64,256]{2,1,0:T(8,128)(2,1)S(1)}, bf16[4,64,256]{2,1,0:T(8,128)(2,1)S(1)}, u32[]{:S(2)}, u32[]{:S(2)}) collective-permute-start(bf16[4,64,256]{2,1,0:T(8,128)(2,1)S(1)} %constant_dynamic-slice_fusion), channel_id=1, source_target_pairs={{0,4},{4,8},{8,12},{12,16},{16,20},{20,24},{24,28},{28,32},{32,36}... | collective-permute-start | bytes 393224 | tf_op jit(solution)/shard_map/ppermute | solution.py:106
  5.5 0.1 fusion
  5.6 0.6 %copy-done.5 = s32[32,8]{0,1:T(8,128)S(1)} copy-done((s32[32,8]{0,1:T(8,128)S(1)}, s32[32,8]{0,1:T(8,128)}, u32[]{:S(2)}) %copy-start.5) | copy-done | bytes 1048
  6.2 0.1 dynamic-slice_subtract_fusion
  6.3 0.6 %copy-done.4 = s32[1024]{0:T(1024)S(1)} copy-done((s32[1024]{0:T(1024)S(1)}, s32[1024]{0:T(1024)}, u32[]{:S(2)}) %copy-start.4) | copy-done | bytes 4120
  6.9 0.1 fusion.2
  7.0 0.1 copy.11
  7.0 0.1 reshape.11.idx_ref
  7.1 0.1 select_reduce_fusion
  7.2 0.1 copy.10
  7.3 0.1 reshape.10.slot_ref
  7.4 9.8 %collective-permute-done.halo_ref = bf16[4,64,256]{2,1,0:T(8,128)(2,1)S(1)} collective-permute-done((bf16[4,64,256]{2,1,0:T(8,128)(2,1)S(1)}, bf16[4,64,256]{2,1,0:T(8,128)(2,1)S(1)}, u32[]{:S(2)}, u32[]{:S(2)}) %collective-permute-start) | collective-permute-done | bytes 131104 | tf_op jit(solution)/shard_map/ppermute | solution.py:106
  17.2 1.2 %copy-done = bf16[32,64,256]{2,1,0:T(8,128)(2,1)S(1)} copy-done((bf16[32,64,256]{2,1,0:T(8,128)(2,1)S(1)}, bf16[32,64,256]{2,1,0:T(8,128)(2,1)}, u32[]{:S(2)}) %copy-start) | copy-done | bytes 1048600
  18.5 1.0 %copy-done.1 = bf16[8,64,512]{2,1,0:T(8,128)(2,1)S(1)} copy-done((bf16[8,64,512]{2,1,0:T(8,128)(2,1)S(1)}, bf16[8,64,512]{2,1,0:T(8,128)(2,1)}, u32[]{:S(2)}) %copy-start.1) | copy-done | bytes 524312
  19.5 2.5 %terms.1 = (f32[4,256,128]{2,1,0:T(8,128)S(1)}, bf16[4,256,128]{2,1,0:T(8,128)(2,1)S(1)}) custom-call(s32[64]{0:T(128)S(1)} %reshape.10.slot_ref, s32[64]{0:T(128)S(1)} %reshape.11.idx_ref, s32[1]{0:T(128)} %bitcast.g_ref, bf16[8,64,512]{2,1,0:T(8,128)(2,1)S(1)} %copy-done.1, bf16[32,64,256]{2,1,0:T(8,128)(2,1)S(1)} %copy-done, ...), custom_call_target="tpu_custom_call" | custom-call | tf_op jit(solution)/shard_map/terms/pallas_call | solution.py:120
  22.0 1.9 %collective-permute-start.1 = (bf16[4,256,128]{2,1,0:T(8,128)(2,1)S(1)}, bf16[4,256,128]{2,1,0:T(8,128)(2,1)S(1)}, u32[]{:S(2)}, u32[]{:S(2)}) collective-permute-start(bf16[4,256,128]{2,1,0:T(8,128)(2,1)S(1)} %get-tuple-element.8), channel_id=1, source_target_pairs={{4,3},{8,7},{12,11},{16,15},{20,19},{24,23},{28,27},{32,31},{36,35... | collective-permute-start | bytes 786440 | tf_op jit(solution)/shard_map/ppermute | solution.py:138
  23.9 7.0 %collective-permute-done.1 = bf16[4,256,128]{2,1,0:T(8,128)(2,1)S(1)} collective-permute-done((bf16[4,256,128]{2,1,0:T(8,128)(2,1)S(1)}, bf16[4,256,128]{2,1,0:T(8,128)(2,1)S(1)}, u32[]{:S(2)}, u32[]{:S(2)}) %collective-permute-start.1) | collective-permute-done | bytes 262176 | tf_op jit(solution)/shard_map/ppermute | solution.py:138
  30.9 0.8 %add_convert_fusion = bf16[4,256,128]{2,1,0:T(8,128)(2,1)} fusion(f32[4,256,128]{2,1,0:T(8,128)S(1)} %get-tuple-element.7, bf16[4,256,128]{2,1,0:T(8,128)(2,1)S(1)} %collective-permute-done.1), kind=kLoop, calls=%fused_computation | loop fusion | flops 393216 | bytes 1048576 | tf_op jit(solution)/shard_map/convert_element_type | solution.py:139
  31.7 3.4 %all-to-all-start = ((bf16[4,256,128]{2,1,0:T(8,128)(2,1)}), bf16[4,256,128]{2,1,0:T(8,128)(2,1)S(1)}, u32[]{:S(2)}, u32[]{:S(2)}) async-start(bf16[4,256,128]{2,1,0:T(8,128)(2,1)} %add_convert_fusion), calls=%async_computation | async-start | bytes 524288 | tf_op jit(solution)/shard_map/all_to_all | solution.py:140
  35.1 0.7 %slice.3.pos_ref = s32[4]{0:T(128)} slice(s32[12]{0:T(128)S(1)} %get-tuple-element.10), slice={[4:8]} | slice | bytes 32 | tf_op jit(solution)/shard_map/slice | solution.py:149
  35.7 5.0 %all-to-all-done.got_ref = bf16[4,256,128]{2,1,0:T(8,128)(2,1)S(1)} async-done(((bf16[4,256,128]{2,1,0:T(8,128)(2,1)}), bf16[4,256,128]{2,1,0:T(8,128)(2,1)S(1)}, u32[]{:S(2)}, u32[]{:S(2)}) %all-to-all-start) | async-done | bytes 262176 | tf_op jit(solution)/shard_map/all_to_all | solution.py:140
  40.7 0.7 %copy-done.2 = bf16[4,256,128]{2,1,0:T(8,128)(2,1)} copy-done((bf16[4,256,128]{2,1,0:T(8,128)(2,1)}, bf16[4,256,128]{2,1,0:T(8,128)(2,1)S(1)}, u32[]{:S(2)}) %copy-start.2) | copy-done | bytes 262168
  41.4 1.8 %final.1 = f32[4,64,192]{2,1,0:T(8,128)} custom-call(s32[4]{0:T(128)} %slice.3.pos_ref, bf16[4,256,128]{2,1,0:T(8,128)(2,1)} %copy-done.2), custom_call_target="tpu_custom_call" | custom-call | tf_op jit(solution)/shard_map/final/pallas_call | solution.py:142
  (7 shorter events, 0.0 us)
Async XLA Ops:
  0.0 5.5 %copy-start.3 = (s32[8192,4]{0,1:T(4,128)S(1)}, s32[8192,4]{0,1:T(4,128)}, u32[]{:S(2)}) copy-start(s32[8192,4]{0,1:T(4,128)} %param.8) | copy-start | bytes 393220
  1.0 16.3 %collective-permute-start = (bf16[4,64,256]{2,1,0:T(8,128)(2,1)S(1)}, bf16[4,64,256]{2,1,0:T(8,128)(2,1)S(1)}, u32[]{:S(2)}, u32[]{:S(2)}) collective-permute-start(bf16[4,64,256]{2,1,0:T(8,128)(2,1)S(1)} %constant_dynamic-slice_fusion), channel_id=1, source_target_pairs={{0,4},{4,8},{8,12},{12,16},{16,20},{20,24},{24,28},{28,32},{32,36}... | collective-permute-start | bytes 393224 | tf_op jit(solution)/shard_map/ppermute | solution.py:106
  5.5 0.7 %copy-start.5 = (s32[32,8]{0,1:T(8,128)S(1)}, s32[32,8]{0,1:T(8,128)}, u32[]{:S(2)}) copy-start(s32[32,8]{0,1:T(8,128)} %param.6) | copy-start | bytes 3076
  6.2 0.7 %copy-start.4 = (s32[1024]{0:T(1024)S(1)}, s32[1024]{0:T(1024)}, u32[]{:S(2)}) copy-start(s32[1024]{0:T(1024)} %param.9) | copy-start | bytes 12292
  17.2 1.2 %copy-start = (bf16[32,64,256]{2,1,0:T(8,128)(2,1)S(1)}, bf16[32,64,256]{2,1,0:T(8,128)(2,1)}, u32[]{:S(2)}) copy-start(bf16[32,64,256]{2,1,0:T(8,128)(2,1)} %p_ref.1) | copy-start | bytes 3145732
  18.5 1.0 %copy-start.1 = (bf16[8,64,512]{2,1,0:T(8,128)(2,1)S(1)}, bf16[8,64,512]{2,1,0:T(8,128)(2,1)}, u32[]{:S(2)}) copy-start(bf16[8,64,512]{2,1,0:T(8,128)(2,1)} %a_ref.1) | copy-start | bytes 1572868
  22.0 8.9 %collective-permute-start.1 = (bf16[4,256,128]{2,1,0:T(8,128)(2,1)S(1)}, bf16[4,256,128]{2,1,0:T(8,128)(2,1)S(1)}, u32[]{:S(2)}, u32[]{:S(2)}) collective-permute-start(bf16[4,256,128]{2,1,0:T(8,128)(2,1)S(1)} %get-tuple-element.8), channel_id=1, source_target_pairs={{4,3},{8,7},{12,11},{16,15},{20,19},{24,23},{28,27},{32,31},{36,35... | collective-permute-start | bytes 786440 | tf_op jit(solution)/shard_map/ppermute | solution.py:138
  31.7 9.1 %all-to-all-start = ((bf16[4,256,128]{2,1,0:T(8,128)(2,1)}), bf16[4,256,128]{2,1,0:T(8,128)(2,1)S(1)}, u32[]{:S(2)}, u32[]{:S(2)}) async-start(bf16[4,256,128]{2,1,0:T(8,128)(2,1)} %add_convert_fusion), calls=%async_computation | async-start | bytes 524288 | tf_op jit(solution)/shard_map/all_to_all | solution.py:140
  40.7 0.7 %copy-start.2 = (bf16[4,256,128]{2,1,0:T(8,128)(2,1)}, bf16[4,256,128]{2,1,0:T(8,128)(2,1)S(1)}, u32[]{:S(2)}) copy-start(bf16[4,256,128]{2,1,0:T(8,128)(2,1)S(1)} %all-to-all-done.got_ref) | copy-start | bytes 786436

commit v2 on v1

v2 whole, which is shorter than its diff:
```python
import jax
import jax.numpy as jnp
from jax import lax
from jax.experimental import pallas as pl
from jax.experimental.pallas import tpu as pltpu
from jax.sharding import PartitionSpec as P

B = 64
KA = 8
KP = 4
HB = 4
LANES = 2 * B
VMEM = pl.BlockSpec(memory_space=pltpu.VMEM)
SMEM = pl.BlockSpec(memory_space=pltpu.SMEM)


def spread_row(x, slot_ref, base, groups, left):
    x = x.astype(jnp.float32)
    pieces = []
    for v in range(KP // 2):
        pair = x[:, v * LANES : (v + 1) * LANES]
        turned = pltpu.roll(pair, B, 1)
        pieces.append((pair, turned, slot_ref[base + 2 * v], slot_ref[base + 2 * v + 1]))
    out = []
    for c in range(groups):
        total = None
        for pair, turned, s0, s1 in pieces:
            def flag(s, w):
                return (s == w).astype(jnp.float32)
            keep = jnp.where(left, flag(s0, 2 * c), flag(s1, 2 * c + 1))
            swap = jnp.where(left, flag(s1, 2 * c), flag(s0, 2 * c + 1))
            term = pair * keep + turned * swap
            total = term if total is None else total + term
        out.append(total.astype(jnp.bfloat16))
    return out


def spread_rows(load, slot_ref, pd_ref, first, count, groups, left, below=0):
    for t in range(count):
        row = first + t
        for c, block in enumerate(spread_row(load(t), slot_ref, row * KP, groups, left)):
            rows = pl.ds(pl.multiple_of((row - below) * B, B), B)
            pd_ref[rows, c * LANES : (c + 1) * LANES] = block


def ap_row(a, idx_ref, base, pd_ref, below=0):
    picked = jnp.concatenate(
        [pd_ref[pl.ds(pl.multiple_of((idx_ref[base + k] - below) * B, B), B), :] for k in range(KA)], axis=0
    )
    return jnp.dot(a, picked, preferred_element_type=jnp.float32).astype(jnp.bfloat16)


def left_half():
    return lax.broadcasted_iota(jnp.int32, (1, LANES), 1) < B


def own_kernel(slot_ref, idx_ref, g_ref, a_ref, p_ref, pd_ref, ap_ref):
    groups = pd_ref.shape[1] // LANES
    count = a_ref.shape[0]
    fine = p_ref.shape[0]
    g = g_ref[0]

    def load(t):
        return p_ref[jnp.clip(count * g - HB + t, 0, fine - 1)]

    spread_rows(load, slot_ref, pd_ref, HB, count + 2 * HB, groups, left_half(), HB)
    for i in range(count):
        ap_ref[i * B : (i + 1) * B, :] = ap_row(a_ref[i], idx_ref, i * KA, pd_ref, HB)


def edge_kernel(
    slot_ref, idx_ref, far_ref, g_ref, pos_ref, a_ref, far_a_ref, far_p_ref, own_pd_ref, own_ap_ref,
    sent_ref, pd_ref, ap_ref,
):
    groups = sent_ref.shape[0]
    count = a_ref.shape[0]
    g = g_ref[0]
    lower = g < groups // 2
    low_edge = g == 0
    pd_ref[HB * B : (count + 3 * HB) * B, :] = own_pd_ref[...]
    ap_ref[HB * B : (count + HB) * B, :] = own_ap_ref[...]

    @pl.when(jnp.logical_or(low_edge, g == groups - 1))
    def _():
        first = jnp.where(low_edge, 0, count + 2 * HB)
        spread_rows(lambda t: far_p_ref[t], slot_ref, pd_ref, first, 2 * HB, groups, left_half())
        own = jnp.where(low_edge, 0, count - HB)
        far = jnp.where(low_edge, 0, count + HB)
        for t in range(HB):
            rows = pl.ds(pl.multiple_of((HB + own + t) * B, B), B)
            ap_ref[rows, :] = ap_row(a_ref[own + t], idx_ref, (own + t) * KA, pd_ref)
            rows = pl.ds(pl.multiple_of((far + t) * B, B), B)
            ap_ref[rows, :] = ap_row(far_a_ref[t * B : (t + 1) * B, :], far_ref, t * KA, pd_ref)

    @pl.when(jnp.logical_and(g > 0, g < groups - 1))
    def _():
        zeros = jnp.zeros((HB * B, groups * LANES), jnp.bfloat16)
        ap_ref[0 : HB * B, :] = zeros
        ap_ref[(count + HB) * B :, :] = zeros

    first = jnp.where(lower, 0, HB)
    size = (count + HB) * B
    terms = lax.dot_general(
        pd_ref[pl.ds(pl.multiple_of((HB + first) * B, B), size), :],
        ap_ref[pl.ds(pl.multiple_of(first * B, B), size), :],
        (((0,), (0,)), ((), ())),
        preferred_element_type=jnp.float32,
    )
    for place in range(groups):
        one = terms[2 * place * B : (2 * place + 1) * B]
        two = terms[(2 * place + 1) * B : (2 * place + 2) * B]
        own = jnp.where(lower, two, one).astype(jnp.bfloat16)
        h = jnp.int32(0)
        for other in range(1, groups):
            h += jnp.where(pos_ref[other] == place, other, 0)
        rows = pl.ds(pl.multiple_of(h * B, B), B)
        for c in range(groups):
            sent_ref[c, rows, :] = own[:, c * LANES : (c + 1) * LANES]


def on_device(a_vals, a_cols, p_vals, p_cols, colpos):
    groups = lax.axis_size("cols")
    parts = lax.axis_size("rows")
    g = lax.axis_index("cols")
    p = lax.axis_index("rows")
    count = a_vals.shape[0]
    fine = p_vals.shape[0]
    coarse = groups
    last = groups - 1
    table = count + 4 * HB
    start = p * fine + g * count

    sent_p = lax.dynamic_slice_in_dim(p_vals, jnp.where(g < groups // 2, fine - 2 * HB, 0), 2 * HB, 0)
    pairs = [(q * groups + 1, (q + 1) * groups) for q in range(parts - 1)]
    pairs += [((q + 1) * groups + last - 1, q * groups + last) for q in range(parts - 1)]
    far_p = lax.ppermute(sent_p, ("rows", "cols"), pairs)

    own_cols = lax.dynamic_slice_in_dim(a_cols, g * count, count, 0)
    edge_row = jnp.where(g == 0, 0, count - HB)
    edge_a = lax.dynamic_slice_in_dim(a_vals, edge_row, HB, 0).reshape(HB * B, KA * B)
    steps = lax.dynamic_slice_in_dim(own_cols, edge_row, HB, 0) + HB
    steps = steps - (start + edge_row + jnp.arange(HB, dtype=jnp.int32))[:, None]
    steps = steps.reshape(1, HB * KA).astype(jnp.bfloat16)
    steps = jnp.pad(steps, ((0, 15), (0, KA * B - HB * KA)))
    pairs = [(q * groups, (q - 1) * groups + last) for q in range(1, parts)]
    pairs += [(target, source) for source, target in pairs]
    far_a = lax.ppermute(jnp.concatenate([edge_a, steps], axis=0), ("rows", "cols"), pairs)

    pad = 2 * HB
    near_cols = lax.dynamic_slice_in_dim(jnp.pad(p_cols, ((pad, pad), (0, 0))), start, table, 0)
    win_pos = lax.dynamic_slice_in_dim(jnp.pad(colpos, (coarse, coarse)), p * coarse, 3 * coarse, 0)
    relative = near_cols - (p - 1) * coarse
    match = relative[:, :, None] == jnp.arange(3 * coarse, dtype=jnp.int32)
    place = 2 * win_pos + jnp.arange(3 * coarse, dtype=jnp.int32) // coarse
    first_band = jnp.where(g < groups // 2, 0, 1)
    slots = jnp.sum(jnp.where(match, place - first_band, 0), axis=2).reshape(-1)
    local = (own_cols - (start - pad)).reshape(-1)
    own_pos = win_pos[coarse : 2 * coarse]
    which = jnp.reshape(g, (1,))

    pd, ap = pl.pallas_call(
        own_kernel,
        out_shape=(
            jax.ShapeDtypeStruct(((count + 2 * HB) * B, groups * LANES), jnp.bfloat16),
            jax.ShapeDtypeStruct((count * B, groups * LANES), jnp.bfloat16),
        ),
        in_specs=[SMEM, SMEM, SMEM, VMEM, VMEM],
        out_specs=(VMEM, VMEM),
        compiler_params=pltpu.CompilerParams(vmem_limit_bytes=24 << 20),
        cost_estimate=pl.CostEstimate(flops=1 << 31, bytes_accessed=4 << 20, transcendentals=0),
        name="own_rows",
    )(slots, local, which, a_vals, p_vals)

    far_steps = far_a[HB * B, : HB * KA].astype(jnp.int32)
    far_steps = far_steps + jnp.arange(HB * KA, dtype=jnp.int32) // KA
    far_local = far_steps + jnp.where(g == 0, 0, count + HB)
    sent = pl.pallas_call(
        edge_kernel,
        out_shape=jax.ShapeDtypeStruct((groups, coarse * B, LANES), jnp.bfloat16),
        in_specs=[SMEM] * 5 + [VMEM] * 5,
        out_specs=VMEM,
        scratch_shapes=[
            pltpu.VMEM((table * B, groups * LANES), jnp.bfloat16),
            pltpu.VMEM(((count + 2 * HB) * B, groups * LANES), jnp.bfloat16),
        ],
        compiler_params=pltpu.CompilerParams(vmem_limit_bytes=24 << 20),
        name="edge_rows",
    )(slots, local, far_local, which, own_pos, a_vals, far_a, far_p, pd, ap)

    got = lax.all_to_all(sent, "cols", 0, 0).astype(jnp.float32)
    half = groups // 2
    low = sum(got[c] for c in range(1, half)) + got[0]
    high = sum(got[c] for c in range(half + 1, groups)) + got[half]
    out = jnp.pad(low, ((0, 0), (0, B))) + jnp.pad(high, ((0, 0), (B, 0)))
    return out.reshape(coarse, B, 3 * B)


def solution(mesh):
    placed = (P(("rows", "cols"), None, None), P("rows", None), P("rows", None, None), P(), P())
    return jax.shard_map(
        on_device, mesh=mesh, in_specs=placed, out_specs=P("rows", None, "cols"), check_vma=False
    )
```

time: 43.6 us -> 32.8 us (0.75)
  the two profiles are of different devices: /device:TPU:1 before, /device:TPU:8 now
where the time goes in v2:
time: 32.8 us; the launch traced here: 32.5 us
  blocking collectives  21.3 us (65%)
  local copies, waits for them, and re-layouts  4.14 us (13%)
  Pallas kernels  3.46 us (11%)
  starting transfers between devices  2.12 us (6%)
  other arithmetic  1.34 us (4%)
    all_to_all x1, blocking collectives, on_device(): got = lax.all_to_all(sent, 'cols', 0, 0).astype(jnp.float32)  21.3 us
    unnamed x10, local copies, waits for them, and re-layouts  2.5 us
    pallas_call x1, Pallas kernels, on_device(): pl.pallas_call(own_kernel, out_shape=(jax.ShapeDtypeStruct(((count + 2 *...  2.14 us
    pallas_call x1, Pallas kernels, on_device(): pl.pallas_call(edge_kernel, out_shape=jax.ShapeDtypeStruct((groups, coars...  1.31 us
    ppermute x1, starting transfers between devices, on_device(): far_p = lax.ppermute(sent_p, ('rows', 'cols'), pairs)  1.31 us
    dynamic_slice x1, local copies, waits for them, and re-layouts, on_device(): lax.dynamic_slice_in_dim(p_vals, jnp.where(g < groups // 2, fine - 2 * HB...  1.03 us
    add x1, other arithmetic, on_device(): out = jnp.pad(low, ((0, 0), (0, B))) + jnp.pad(high, ((0, 0), (B, 0)))  0.84 us
    ppermute x1, starting transfers between devices, on_device(): lax.ppermute(jnp.concatenate([edge_a, steps], axis=0), ('rows', 'cols'),...  0.81 us
  transfers between devices with their start and end apart: 2, of which 0 were waited for; matrix products, arithmetic and copies ran while one was open for 3% of the time, Pallas kernels for 7%

profile of v2, /device:TPU:8, one launch (start us, length us, event | category | flops | bytes accessed | tf_op | source)
XLA Modules:
  0.0 32.5 jit_solution(9018506785723617229)
XLA Ops:
  0.0 1.0 %constant_dynamic-slice_fusion.1 = bf16[8,64,256]{2,1,0:T(8,128)(2,1)S(1)} fusion(bf16[32,64,256]{2,1,0:T(8,128)(2,1)} %p_ref.1, s32[]{:T(128)S(6)} %select_n.54), kind=kLoop, calls=%fused_computation.18 | loop fusion | bytes 524292 | tf_op jit(solution)/shard_map/dynamic_slice | solution.py:133
  1.0 1.3 %collective-permute-start.1 = (bf16[8,64,256]{2,1,0:T(8,128)(2,1)S(1)}, bf16[8,64,256]{2,1,0:T(8,128)(2,1)S(1)}, u32[]{:S(2)}, u32[]{:S(2)}) collective-permute-start(bf16[8,64,256]{2,1,0:T(8,128)(2,1)S(1)} %constant_dynamic-slice_fusion.1), channel_id=1, source_target_pairs={{1,4},{5,8},{9,12},{13,16},{17,20},{21,24},{25,28},{29,32},{33,36}... | collective-permute-start | bytes 786440 | tf_op jit(solution)/shard_map/ppermute | solution.py:136
  2.4 0.0 copy-start.3
  2.4 0.7 %copy-done.3 = s32[32,8]{0,1:T(8,128)S(1)} copy-done((s32[32,8]{0,1:T(8,128)S(1)}, s32[32,8]{0,1:T(8,128)}, u32[]{:S(2)}) %copy-start.3) | copy-done | bytes 1048
  3.1 0.1 subtract_convert_fusion
  3.1 0.1 copy.14
  3.2 0.1 convert_element_type.30
  3.3 0.0 copy-start.2
  3.4 0.8 %collective-permute-start = (bf16[272,512]{1,0:T(8,128)(2,1)S(1)}, bf16[272,512]{1,0:T(8,128)(2,1)S(1)}, u32[]{:S(2)}, u32[]{:S(2)}) collective-permute-start(bf16[272,512]{1,0:T(8,128)(2,1)S(1)} %fusion.1), channel_id=1, source_target_pairs={{4,3},{8,7},{12,11},{16,15},{20,19},{24,23},{28,27},{32,31},{36,35... | collective-permute-start | bytes 835592 | tf_op jit(solution)/shard_map/ppermute | solution.py:147
  4.2 0.1 dynamic-slice_subtract_fusion
  4.3 0.1 copy.13
  4.4 0.1 reshape.39.idx_ref
  4.5 0.6 %copy-done.4 = s32[1024]{0:T(1024)S(1)} copy-done((s32[1024]{0:T(1024)S(1)}, s32[1024]{0:T(1024)}, u32[]{:S(2)}) %copy-start.4) | copy-done | bytes 4120
  5.1 0.1 fusion.6
  5.1 0.1 fusion.4
  5.2 0.1 select_reduce_fusion
  5.3 0.1 copy.12
  5.4 0.1 reshape.38.slot_ref
  5.5 1.2 %copy-done.1 = bf16[32,64,256]{2,1,0:T(8,128)(2,1)S(1)} copy-done((bf16[32,64,256]{2,1,0:T(8,128)(2,1)S(1)}, bf16[32,64,256]{2,1,0:T(8,128)(2,1)}, u32[]{:S(2)}) %copy-start.1) | copy-done | bytes 1048600
  6.7 2.1 %own_rows.1 = (bf16[1024,512]{1,0:T(8,128)(2,1)S(1)}, bf16[512,512]{1,0:T(8,128)(2,1)S(1)}) custom-call(s32[96]{0:T(128)S(1)} %reshape.38.slot_ref, s32[64]{0:T(128)S(1)} %reshape.39.idx_ref, s32[1]{0:T(128)} %bitcast.2.g_ref, bf16[8,64,512]{2,1,0:T(8,128)(2,1)S(1)} %copy-done, bf16[32,64,256]{2,1,0:T(8,128)(2,1)S(1)} %copy-done.1), custom_call_target="tpu_custom_call" | custom-call | flops 2147483648 | bytes 4194304 | tf_op jit(solution)/shard_map/own_rows/pallas_call | solution.py:161
  8.9 0.1 slice.19.pos_ref
  9.0 1.3 %edge_rows.1 = bf16[4,256,128]{2,1,0:T(8,128)(2,1)S(1)} custom-call(s32[96]{0:T(128)S(1)} %reshape.38.slot_ref, s32[64]{0:T(128)S(1)} %reshape.39.idx_ref, s32[32]{0:T(128)S(1)} %fusion.8.far_ref, s32[1]{0:T(128)} %bitcast.2.g_ref, s32[4]{0:T(128)S(1)} %slice.19.pos_ref, bf16[8,64,512]{2,1,0:T(8,128)(2,1)S(1)} %copy-done, ...), custom_call_target="tpu_custom_call" | custom-call | tf_op jit(solution)/shard_map/edge_rows/pallas_call | solution.py:177
  10.3 21.3 %all_to_all.5 = bf16[4,256,128]{2,1,0:T(8,128)(2,1)S(1)} all-to-all(bf16[4,256,128]{2,1,0:T(8,128)(2,1)S(1)} %edge_rows.1), channel_id=1, replica_groups=mesh['rows'=256,'cols'=4] {'cols'}, dimensions={0} | all-to-all | bytes 524288 | tf_op jit(solution)/shard_map/all_to_all | solution.py:190
  31.6 0.8 %pad_add_fusion = f32[256,192]{1,0:T(8,128)} fusion(f32[256,128]{1,0:T(8,128)S(1)} %get-tuple-element.12, f32[256,128]{1,0:T(8,128)S(1)} %get-tuple-element.11), kind=kLoop, calls=%fused_computation.3 | loop fusion | flops 49152 | bytes 458752 | tf_op jit(solution)/shard_map/add | solution.py:194
  (13 shorter events, 0.1 us)
Async XLA Ops:
  0.0 3.3 %copy-start = (bf16[8,64,512]{2,1,0:T(8,128)(2,1)S(1)}, bf16[8,64,512]{2,1,0:T(8,128)(2,1)}, u32[]{:S(2)}) copy-start(bf16[8,64,512]{2,1,0:T(8,128)(2,1)} %a_ref.3) | copy-start | bytes 1572868
  1.0 7.9 %collective-permute-start.1 = (bf16[8,64,256]{2,1,0:T(8,128)(2,1)S(1)}, bf16[8,64,256]{2,1,0:T(8,128)(2,1)S(1)}, u32[]{:S(2)}, u32[]{:S(2)}) collective-permute-start(bf16[8,64,256]{2,1,0:T(8,128)(2,1)S(1)} %constant_dynamic-slice_fusion.1), channel_id=1, source_target_pairs={{1,4},{5,8},{9,12},{13,16},{17,20},{21,24},{25,28},{29,32},{33,36}... | collective-permute-start | bytes 786440 | tf_op jit(solution)/shard_map/ppermute | solution.py:136
  2.4 0.7 %copy-start.3 = (s32[32,8]{0,1:T(8,128)S(1)}, s32[32,8]{0,1:T(8,128)}, u32[]{:S(2)}) copy-start(s32[32,8]{0,1:T(8,128)} %param.6) | copy-start | bytes 3076
  3.3 1.8 %copy-start.2 = (s32[8192,4]{0,1:T(4,128)S(1)}, s32[8192,4]{0,1:T(4,128)}, u32[]{:S(2)}) copy-start(s32[8192,4]{0,1:T(4,128)} %param.8) | copy-start | bytes 393220
  3.4 5.6 %collective-permute-start = (bf16[272,512]{1,0:T(8,128)(2,1)S(1)}, bf16[272,512]{1,0:T(8,128)(2,1)S(1)}, u32[]{:S(2)}, u32[]{:S(2)}) collective-permute-start(bf16[272,512]{1,0:T(8,128)(2,1)S(1)} %fusion.1), channel_id=1, source_target_pairs={{4,3},{8,7},{12,11},{16,15},{20,19},{24,23},{28,27},{32,31},{36,35... | collective-permute-start | bytes 835592 | tf_op jit(solution)/shard_map/ppermute | solution.py:147
  4.4 0.7 %copy-start.4 = (s32[1024]{0:T(1024)S(1)}, s32[1024]{0:T(1024)}, u32[]{:S(2)}) copy-start(s32[1024]{0:T(1024)} %param.9) | copy-start | bytes 12292
  5.5 1.2 %copy-start.1 = (bf16[32,64,256]{2,1,0:T(8,128)(2,1)S(1)}, bf16[32,64,256]{2,1,0:T(8,128)(2,1)}, u32[]{:S(2)}) copy-start(bf16[32,64,256]{2,1,0:T(8,128)(2,1)} %p_ref.1) | copy-start | bytes 3145732

commit v3 on v2

v3 whole, which is shorter than its diff:
```python
import jax
import jax.numpy as jnp
from jax import lax
from jax.experimental import pallas as pl
from jax.experimental.pallas import tpu as pltpu
from jax.sharding import PartitionSpec as P

B = 64
KA = 8
KP = 4
HB = 4
LANES = 2 * B
TILE = 16
VMEM = pl.BlockSpec(memory_space=pltpu.VMEM)
SMEM = pl.BlockSpec(memory_space=pltpu.SMEM)


def block(i):
    return pl.ds(pl.multiple_of(i * B, B), B)


def edge_of(g, p):
    lower = jnp.logical_and(g == 0, p > 0)
    upper = jnp.logical_and(g == lax.axis_size("cols") - 1, p < lax.axis_size("rows") - 1)
    return jnp.logical_or(lower, upper)


def turned_pairs(x):
    x = x.astype(jnp.float32)
    pairs = [x[:, v * LANES : (v + 1) * LANES] for v in range(KP // 2)]
    return [(pair, pltpu.roll(pair, B, 1)) for pair in pairs]


def spread(pairs, slots, pieces, ref, row):
    left = lax.broadcasted_iota(jnp.int32, (1, LANES), 1) < B
    side = jnp.where(left, 0, 1)
    keeps = [jnp.where(left, slots[2 * v], slots[2 * v + 1]) - side for v in range(len(pairs))]
    swaps = [jnp.where(left, slots[2 * v + 1], slots[2 * v]) - side for v in range(len(pairs))]
    for c in range(pieces):
        total = jnp.zeros((B, LANES), jnp.float32)
        for (pair, turned), keep, swap in zip(pairs, keeps, swaps):
            total = jnp.where(keep == 2 * c, pair, jnp.where(swap == 2 * c, turned, total))
        ref[block(row), c * LANES : (c + 1) * LANES] = total.astype(jnp.bfloat16)


def ap_row(a, indices, pd_ref):
    picked = jnp.concatenate([pd_ref[block(i), :] for i in indices], axis=0)
    return jnp.dot(a, picked, preferred_element_type=jnp.float32).astype(jnp.bfloat16)


def transposed_dot(x, y):
    return lax.dot_general(x, y, (((0,), (0,)), ((), ())), preferred_element_type=jnp.float32)


def pack_kernel(at_ref, a_ref, _, msg_ref):
    g, p = lax.axis_index("cols"), lax.axis_index("rows")
    fine = at_ref.shape[1]
    tiles = HB * B // TILE
    first = jnp.where(g == 0, 0, a_ref.shape[0] - tiles)
    msg_ref[:tiles] = a_ref[pl.ds(first, tiles)]
    rows = p * fine + lax.broadcasted_iota(jnp.int32, (KA, fine), 1)
    steps = (at_ref[...] - rows + HB).astype(jnp.float32)
    steps = jnp.concatenate([steps, jnp.zeros((KA, LANES - fine), jnp.float32)], axis=1)
    steps = jnp.concatenate([steps, jnp.zeros((TILE - KA, LANES), jnp.float32)], axis=0)
    msg_ref[tiles] = jnp.zeros((TILE, KA * B), jnp.bfloat16)
    msg_ref[tiles, :, :LANES] = steps.astype(jnp.bfloat16)


def own_kernel(
    at_ref, pos_ref, cols_ref, a_ref, p_ref, pd_ref, pn_ref, part_ref, ints_ref, ap_buf
):
    g, p = lax.axis_index("cols"), lax.axis_index("rows")
    groups = lax.axis_size("cols")
    coarse = groups
    count = a_ref.shape[0]
    fine = p_ref.shape[0]
    near = count + 2 * HB
    start = p * fine + g * count

    edge = edge_of(g, p)
    low = g == 0
    base = 1 - p - jnp.where(g < groups // 2, 0, 1)

    def columns(f):
        return [cols_ref[m, f + 2 * HB] for m in range(KP)]

    def slots_of(cols):
        return [2 * pos_ref[h] + lax.div(h, coarse) + base for h in cols]

    for t in range(2 * HB):
        cols = columns(jnp.where(low, t - 2 * HB, count + t))
        for m, (slot, h) in enumerate(zip(slots_of(cols), cols)):
            ints_ref[t * KP + m] = slot
            ints_ref[(2 * HB + t) * KP + m] = h - p * coarse
    for t in range(HB):
        lane = g * count + jnp.where(low, t, count - HB + t)
        shift = start - jnp.where(low, 2 * HB, 0)
        for k in range(KA):
            ints_ref[4 * HB * KP + t * KA + k] = at_ref[k, lane] - shift

    for j in range(near):
        pairs = turned_pairs(p_ref[jnp.clip(count * g - HB + j, 0, fine - 1)])
        cols = columns(j - HB)
        spread(pairs, slots_of(cols), groups, pd_ref, j)
        if HB <= j < HB + count:
            spread(pairs, [h - p * coarse for h in cols], coarse // 2, pn_ref, j - HB)

    first = jnp.where(jnp.logical_and(edge, low), HB, 0)

    def own_row(t, i):
        picks = [at_ref[k, g * count + i] - (start - HB) for k in range(KA)]
        ap_buf[t * B : (t + 1) * B, :] = ap_row(a_ref[i], picks, pd_ref)

    for t in range(count - HB):
        own_row(t, first + t)

    @pl.when(edge)
    def _():
        size = (count - HB) * B
        rows = pl.ds(pl.multiple_of(first * B, B), size)
        part_ref[...] = transposed_dot(pn_ref[rows, :], ap_buf[:size, :])

    @pl.when(jnp.logical_not(edge))
    def _():
        for t in range(count - HB, count):
            own_row(t, t)
        part_ref[...] = transposed_dot(pn_ref[...], ap_buf[...])


def edge_kernel(
    ints_ref, far_ref, own_a_ref, far_a_ref, far_p_ref, pd_ref, pn_ref, part_ref,
    sent_ref, table, lhs, ap_buf,
):
    g, p = lax.axis_index("cols"), lax.axis_index("rows")
    groups = lax.axis_size("cols")
    edge = edge_of(g, p)
    low = g == 0
    size = HB * B
    tiles = size // TILE
    count = pn_ref.shape[0] // B
    fine = far_ref.shape[1]

    def store(total):
        for c in range(groups):
            sent_ref[c] = total[:, c * LANES : (c + 1) * LANES].astype(jnp.bfloat16)

    def half(second):
        return pl.ds(pl.multiple_of(jnp.where(second, size, 0), size), size)

    @pl.when(edge)
    def _():
        rows = pl.ds(pl.multiple_of(jnp.where(low, 2 * size, 0), size), 2 * size)
        table[rows, :] = pd_ref[size : 3 * size, :]
        lhs[half(low), :] = pn_ref[pl.ds(pl.multiple_of(jnp.where(low, 0, (count - HB) * B), B), size), :]
        shift = jnp.where(low, 0, 2 * HB)
        for t in range(2 * HB):
            slots = [ints_ref[t * KP + m] for m in range(KP)]
            spread(turned_pairs(far_p_ref[t]), slots, groups, table, shift + t)
        for t in range(HB):
            s = jnp.where(low, HB, 0) + t
            slots = [ints_ref[(2 * HB + s) * KP + m] for m in range(KP)]
            spread(turned_pairs(far_p_ref[s]), slots, groups // 2, lhs, jnp.where(low, t, HB + t))
        each = B // TILE
        for t in range(HB):
            a = own_a_ref[t * each : (t + 1) * each].reshape(B, KA * B)
            picks = [ints_ref[4 * HB * KP + t * KA + k] for k in range(KA)]
            ap_buf[block(jnp.where(low, HB + t, t)), :] = ap_row(a, picks, table)
        for t in range(HB):
            a = far_a_ref[t * each : (t + 1) * each].reshape(B, KA * B)
            lane = jnp.where(low, fine - HB, 0) + t
            picks = [far_ref[k, lane] + jnp.where(low, t, HB + t) for k in range(KA)]
            ap_buf[block(jnp.where(low, t, HB + t)), :] = ap_row(a, picks, table)
        store(part_ref[...] + transposed_dot(lhs[...], ap_buf[...]))

    @pl.when(jnp.logical_not(edge))
    def _():
        store(part_ref[...])


def on_device(a_vals, a_cols, p_vals, p_cols, colpos):
    groups = lax.axis_size("cols")
    parts = lax.axis_size("rows")
    count = a_vals.shape[0]
    fine = p_vals.shape[0]
    coarse = groups
    g = lax.axis_index("cols")
    p = lax.axis_index("rows")
    last = groups - 1
    near = count + 2 * HB
    wide = groups * LANES
    tiles = HB * B // TILE
    bf16, f32, i32 = jnp.bfloat16, jnp.float32, jnp.int32
    params = pltpu.CompilerParams(vmem_limit_bytes=16 << 20)
    at = a_cols.T

    msg_p = lax.dynamic_slice_in_dim(p_vals, jnp.where(g < groups // 2, fine - 2 * HB, 0), 2 * HB, 0)
    pairs = [(q * groups + 1, (q + 1) * groups) for q in range(parts - 1)]
    pairs += [((q + 1) * groups + last - 1, q * groups + last) for q in range(parts - 1)]
    far_p = lax.ppermute(msg_p, ("rows", "cols"), pairs)
    msg_a = pl.pallas_call(
        pack_kernel,
        out_shape=jax.ShapeDtypeStruct((tiles + 1, TILE, KA * B), bf16),
        in_specs=[VMEM, VMEM, pl.BlockSpec(memory_space=pl.ANY)],
        out_specs=VMEM,
        compiler_params=params,
        name="pack",
    )(at, a_vals.reshape(count * B // TILE, TILE, KA * B), msg_p)
    pairs = [(q * groups, (q - 1) * groups + last) for q in range(1, parts)]
    pairs += [(target, source) for source, target in pairs]
    far_a = lax.ppermute(msg_a, ("rows", "cols"), pairs)

    pad = 2 * HB
    padded = jnp.pad(p_cols.T, ((0, 0), (pad, pad)))
    near_cols = lax.dynamic_slice_in_dim(padded, p * fine + g * count, count + 2 * pad, 1)
    pd, pn, part, ints = pl.pallas_call(
        own_kernel,
        out_shape=(
            jax.ShapeDtypeStruct((near * B, wide), bf16),
            jax.ShapeDtypeStruct((count * B, coarse * B), bf16),
            jax.ShapeDtypeStruct((coarse * B, wide), f32),
            jax.ShapeDtypeStruct((LANES,), i32),
        ),
        in_specs=[SMEM, SMEM, SMEM, VMEM, VMEM],
        out_specs=(VMEM, VMEM, VMEM, SMEM),
        scratch_shapes=[pltpu.VMEM((count * B, wide), bf16)],
        compiler_params=params,
        cost_estimate=pl.CostEstimate(flops=1 << 31, bytes_accessed=4 << 20, transcendentals=0),
        name="own_rows",
    )(at, colpos, near_cols, a_vals, p_vals)

    far_steps = far_a[tiles, :KA, :fine].astype(i32)
    sent = pl.pallas_call(
        edge_kernel,
        out_shape=jax.ShapeDtypeStruct((groups, coarse * B, LANES), bf16),
        in_specs=[SMEM] * 2 + [VMEM] * 6,
        out_specs=VMEM,
        scratch_shapes=[
            pltpu.VMEM((near * B, wide), bf16),
            pltpu.VMEM((2 * HB * B, coarse * B), bf16),
            pltpu.VMEM((2 * HB * B, wide), bf16),
        ],
        compiler_params=params,
        name="edge_rows",
    )(ints, far_steps, msg_a, far_a, far_p, pd, pn, part)

    got = lax.all_to_all(sent, "cols", 0, 0).astype(f32)
    half = groups // 2
    low = sum(got[c] for c in range(1, half)) + got[0]
    high = sum(got[c] for c in range(half + 1, groups)) + got[half]
    out = jnp.pad(low, ((0, 0), (0, B))) + jnp.pad(high, ((0, 0), (B, 0)))
    return out.reshape(coarse, B, 3 * B)


def solution(mesh):
    placed = (P(("rows", "cols"), None, None), P("rows", None), P("rows", None, None), P(), P())
    return jax.shard_map(
        on_device, mesh=mesh, in_specs=placed, out_specs=P("rows", None, "cols"), check_vma=False
    )
```

time: 32.8 us -> 29.9 us (0.912)
  local copies, waits for them, and re-layouts: 4.14 us -> 2.56 us
  blocking collectives: 21.3 us -> 20.1 us
  Pallas kernels: 3.46 us -> 4.05 us
  other arithmetic: 1.34 us -> 0.91 us
    unnamed x10, local copies, waits for them, and re-layouts: 2.5 us -> 0.7 us
    pallas_call x1 -> x2, Pallas kernels: 2.14 us -> 3.39 us  [the longest x1 3.37 us: on_device(): pl.pallas_call(own_kernel, out_shape=(jax.ShapeDtypeStruct((near * B, wid...]
    all_to_all x1, blocking collectives: 21.3 us -> 20.1 us  [on_device(): got = lax.all_to_all(sent, 'cols', 0, 0).astype(f32)]
    dynamic_slice x1, local copies, waits for them, and re-layouts: 0.02 us -> 0.77 us  [on_device(): lax.dynamic_slice_in_dim(padded, p * fine + g * count, count + 2 * pad, 1)]
    pallas_call x1, Pallas kernels: 1.31 us -> 0.66 us  [on_device(): pl.pallas_call(edge_kernel, out_shape=jax.ShapeDtypeStruct((groups, coars...]
  transfers between devices with their start and end apart: 2 -> 2, of which waited for: 0 -> 0; matrix products, arithmetic and copies ran while one was open for 3% -> 3% of each run, Pallas kernels for 7% -> 11%
where the time goes in v3:
time: 29.9 us; the launch traced here: 29.7 us
  blocking collectives  20.1 us (67%)
  Pallas kernels  4.05 us (14%)
  local copies, waits for them, and re-layouts  2.56 us (9%)
  starting transfers between devices  1.98 us (7%)
  other arithmetic  0.91 us (3%)
    all_to_all x1, blocking collectives, on_device(): got = lax.all_to_all(sent, 'cols', 0, 0).astype(f32)  20.1 us
    pallas_call x1, Pallas kernels, on_device(): pl.pallas_call(own_kernel, out_shape=(jax.ShapeDtypeStruct((near * B, wid...  3.37 us
    ppermute x1, starting transfers between devices, on_device(): far_p = lax.ppermute(msg_p, ('rows', 'cols'), pairs)  1.31 us
    dynamic_slice x1, local copies, waits for them, and re-layouts, on_device(): lax.dynamic_slice_in_dim(p_vals, jnp.where(g < groups // 2, fine - 2 * HB...  1.09 us
    add x1, other arithmetic, on_device(): out = jnp.pad(low, ((0, 0), (0, B))) + jnp.pad(high, ((0, 0), (B, 0)))  0.84 us
    dynamic_slice x1, local copies, waits for them, and re-layouts, on_device(): lax.dynamic_slice_in_dim(padded, p * fine + g * count, count + 2 * pad, 1)  0.77 us
    unnamed x10, local copies, waits for them, and re-layouts  0.7 us
    ppermute x1, starting transfers between devices, on_device(): far_a = lax.ppermute(msg_a, ('rows', 'cols'), pairs)  0.68 us
  transfers between devices with their start and end apart: 2, of which 0 were waited for; matrix products, arithmetic and copies ran while one was open for 3% of the time, Pallas kernels for 11%

profile of v3, /device:TPU:8, one launch (start us, length us, event | category | flops | bytes accessed | tf_op | source)
XLA Modules:
  0.0 29.7 jit_solution(10203154886467620051)
XLA Ops:
  0.0 0.0 copy-start
  0.0 0.0 copy-start.1
  0.0 1.1 %constant_dynamic-slice_fusion._ = bf16[8,64,256]{2,1,0:T(8,128)(2,1)S(1)} fusion(bf16[32,64,256]{2,1,0:T(8,128)(2,1)} %p_ref.1, s32[]{:T(128)S(6)} %select_n.9), kind=kLoop, calls=%fused_computation.8 | loop fusion | bytes 524292 | tf_op jit(solution)/shard_map/dynamic_slice | solution.py:196
  1.1 1.3 %collective-permute-start.1 = (bf16[8,64,256]{2,1,0:T(8,128)(2,1)S(1)}, bf16[8,64,256]{2,1,0:T(8,128)(2,1)S(1)}, u32[]{:S(2)}, u32[]{:S(2)}) collective-permute-start(bf16[8,64,256]{2,1,0:T(8,128)(2,1)S(1)} %constant_dynamic-slice_fusion._), channel_id=1, source_target_pairs={{1,4},{5,8},{9,12},{13,16},{17,20},{21,24},{25,28},{29,32},{33,36}... | collective-permute-start | bytes 786440 | tf_op jit(solution)/shard_map/ppermute | solution.py:199
  2.4 0.0 copy-done
  2.4 0.0 copy-start.2
  2.4 0.7 %copy-done.2 = s32[32,8]{0,1:T(8,128)S(1)} copy-done((s32[32,8]{0,1:T(8,128)S(1)}, s32[32,8]{0,1:T(8,128)}, u32[]{:S(2)}) %copy-start.2) | copy-done | bytes 1048
  3.1 0.7 %collective-permute-start = (bf16[17,16,512]{2,1,0:T(8,128)(2,1)S(1)}, bf16[17,16,512]{2,1,0:T(8,128)(2,1)S(1)}, u32[]{:S(2)}, u32[]{:S(2)}) collective-permute-start(bf16[17,16,512]{2,1,0:T(8,128)(2,1)S(1)} %pack.1.own_a_ref), channel_id=1, source_target_pairs={{4,3},{8,7},{12,11},{16,15},{20,19},{24,23},{28,27},{32,31},{36,35... | collective-permute-start | bytes 835592 | tf_op jit(solution)/shard_map/ppermute | solution.py:210
  3.8 0.0 copy-start.3
  3.8 0.0 copy-start.4
  3.8 0.8 %pad_dynamic-slice_fusion.cols_ref = s32[4,24]{1,0:T(4,128)S(1)} fusion(s32[]{:T(128)S(6)} %select_n.8, s32[4,8192]{1,0:T(4,128)} %bitcast.16), kind=kLoop, calls=%fused_computation.1 | loop fusion | bytes 131460 | tf_op jit(solution)/shard_map/dynamic_slice | solution.py:214
  4.6 0.0 copy-done.1
  4.6 0.0 copy-done.3
  4.6 0.0 copy-done.4
  4.6 3.4 %own_rows.1 = (bf16[1024,512]{1,0:T(8,128)(2,1)S(1)}, bf16[512,256]{1,0:T(8,128)(2,1)S(1)}, f32[256,512]{1,0:T(8,128)S(1)}, s32[128]{0:T(128)S(1)}) custom-call(s32[8,32]{1,0:T(8,128)S(1)} %bitcast.15, s32[1024]{0:T(1024)S(1)} %copy-done.4, s32[4,24]{1,0:T(4,128)S(1)} %pad_dynamic-slice_fusion.cols_ref, bf16[8,64,512]{2,1,0:T(8,128)(2,1)S(1)} %copy-done, ...), custom_call_target="tpu_custom_call" | custom-call | flops 2147483648 | bytes 4194304 | tf_op jit(solution)/shard_map/own_rows/pallas_call | solution.py:215
  8.0 0.0 collective-permute-done.far_a_ref
  8.0 0.0 collective-permute-done.1.far_p_ref
  8.0 0.7 %edge_rows.1 = bf16[4,256,128]{2,1,0:T(8,128)(2,1)S(1)} custom-call(s32[128]{0:T(128)S(1)} %get-tuple-element.9.ints_ref, s32[8,32]{1,0:T(8,128)S(1)} %fusion.2.far_ref, bf16[17,16,512]{2,1,0:T(8,128)(2,1)S(1)} %pack.1.own_a_ref, bf16[17,16,512]{2,1,0:T(8,128)(2,1)S(1)} %collective-permute-done.far_a_ref, ...), custom_call_target="tpu_custom_call" | custom-call | tf_op jit(solution)/shard_map/edge_rows/pallas_call | solution.py:232
  8.7 20.1 %all_to_all.5 = bf16[4,256,128]{2,1,0:T(8,128)(2,1)S(1)} all-to-all(bf16[4,256,128]{2,1,0:T(8,128)(2,1)S(1)} %edge_rows.1), channel_id=1, replica_groups=mesh['rows'=256,'cols'=4] {'cols'}, dimensions={0} | all-to-all | bytes 524288 | tf_op jit(solution)/shard_map/all_to_all | solution.py:246
  28.9 0.8 %pad_add_fusion = f32[256,192]{1,0:T(8,128)} fusion(f32[256,128]{1,0:T(8,128)S(1)} %get-tuple-element.14, f32[256,128]{1,0:T(8,128)S(1)} %get-tuple-element.13), kind=kLoop, calls=%fused_computation | loop fusion | flops 49152 | bytes 458752 | tf_op jit(solution)/shard_map/add | solution.py:250
  (4 shorter events, 0.1 us)
Async XLA Ops:
  0.0 2.4 %copy-start = (bf16[8,64,512]{2,1,0:T(8,128)(2,1)S(1)}, bf16[8,64,512]{2,1,0:T(8,128)(2,1)}, u32[]{:S(2)}) copy-start(bf16[8,64,512]{2,1,0:T(8,128)(2,1)} %a_ref.1) | copy-start | bytes 1572868
  0.0 4.6 %copy-start.1 = (bf16[32,64,256]{2,1,0:T(8,128)(2,1)S(1)}, bf16[32,64,256]{2,1,0:T(8,128)(2,1)}, u32[]{:S(2)}) copy-start(bf16[32,64,256]{2,1,0:T(8,128)(2,1)} %p_ref.1) | copy-start | bytes 3145732
  1.1 6.9 %collective-permute-start.1 = (bf16[8,64,256]{2,1,0:T(8,128)(2,1)S(1)}, bf16[8,64,256]{2,1,0:T(8,128)(2,1)S(1)}, u32[]{:S(2)}, u32[]{:S(2)}) collective-permute-start(bf16[8,64,256]{2,1,0:T(8,128)(2,1)S(1)} %constant_dynamic-slice_fusion._), channel_id=1, source_target_pairs={{1,4},{5,8},{9,12},{13,16},{17,20},{21,24},{25,28},{29,32},{33,36}... | collective-permute-start | bytes 786440 | tf_op jit(solution)/shard_map/ppermute | solution.py:199
  2.4 0.7 %copy-start.2 = (s32[32,8]{0,1:T(8,128)S(1)}, s32[32,8]{0,1:T(8,128)}, u32[]{:S(2)}) copy-start(s32[32,8]{0,1:T(8,128)} %param.6) | copy-start | bytes 3076
  3.1 4.9 %collective-permute-start = (bf16[17,16,512]{2,1,0:T(8,128)(2,1)S(1)}, bf16[17,16,512]{2,1,0:T(8,128)(2,1)S(1)}, u32[]{:S(2)}, u32[]{:S(2)}) collective-permute-start(bf16[17,16,512]{2,1,0:T(8,128)(2,1)S(1)} %pack.1.own_a_ref), channel_id=1, source_target_pairs={{4,3},{8,7},{12,11},{16,15},{20,19},{24,23},{28,27},{32,31},{36,35... | collective-permute-start | bytes 835592 | tf_op jit(solution)/shard_map/ppermute | solution.py:210
  3.8 0.8 %copy-start.3 = (s32[32,8]{0,1:T(8,128)S(1)}, s32[32,8]{0,1:T(8,128)}, u32[]{:S(2)}) copy-start(s32[32,8]{0,1:T(8,128)} %param.6) | copy-start | bytes 3076
  3.8 0.8 %copy-start.4 = (s32[1024]{0:T(1024)S(1)}, s32[1024]{0:T(1024)}, u32[]{:S(2)}) copy-start(s32[1024]{0:T(1024)} %pos_ref.1) | copy-start | bytes 12292

commit v4 on v3

v4 whole, which is shorter than its diff:
```python
import jax
import jax.numpy as jnp
from jax import lax
from jax.experimental import pallas as pl
from jax.experimental.pallas import tpu as pltpu
from jax.sharding import PartitionSpec as P

B = 64
KA = 8
KP = 4
HB = 4
LANES = 2 * B
VMEM = pl.BlockSpec(memory_space=pltpu.VMEM)
SMEM = pl.BlockSpec(memory_space=pltpu.SMEM)


def block(i):
    return pl.ds(pl.multiple_of(i * B, B), B)


def edge_of(g, p):
    lower = jnp.logical_and(g == 0, p > 0)
    upper = jnp.logical_and(g == lax.axis_size("cols") - 1, p < lax.axis_size("rows") - 1)
    return jnp.logical_or(lower, upper)


def turned_pairs(x):
    x = x.astype(jnp.float32)
    pairs = [x[:, v * LANES : (v + 1) * LANES] for v in range(KP // 2)]
    return [(pair, pltpu.roll(pair, B, 1)) for pair in pairs]


def spread(pairs, slots, pieces, ref, row):
    left = lax.broadcasted_iota(jnp.int32, (1, LANES), 1) < B
    side = jnp.where(left, 0, 1)
    keeps = [jnp.where(left, slots[2 * v], slots[2 * v + 1]) - side for v in range(len(pairs))]
    swaps = [jnp.where(left, slots[2 * v + 1], slots[2 * v]) - side for v in range(len(pairs))]
    for c in range(pieces):
        total = jnp.zeros((B, LANES), jnp.float32)
        for (pair, turned), keep, swap in zip(pairs, keeps, swaps):
            total = jnp.where(keep == 2 * c, pair, jnp.where(swap == 2 * c, turned, total))
        ref[block(row), c * LANES : (c + 1) * LANES] = total.astype(jnp.bfloat16)


def ap_row(a, indices, pd_ref):
    picked = jnp.concatenate([pd_ref[block(i), :] for i in indices], axis=0)
    return jnp.dot(a, picked, preferred_element_type=jnp.float32).astype(jnp.bfloat16)


def transposed_dot(x, y):
    return lax.dot_general(x, y, (((0,), (0,)), ((), ())), preferred_element_type=jnp.float32)


def pack_kernel(a_ref, _, msg_ref):
    first = jnp.where(lax.axis_index("cols") == 0, 0, a_ref.shape[0] - HB)
    msg_ref[...] = a_ref[pl.ds(first, HB)]


def lookups(pos_ref, cols_ref):
    g, p = lax.axis_index("cols"), lax.axis_index("rows")
    coarse = groups = lax.axis_size("cols")
    base = 1 - p - jnp.where(g < groups // 2, 0, 1)

    def columns(f):
        return [cols_ref[m, f + 2 * HB] for m in range(KP)]

    def slots_of(cols):
        return [2 * pos_ref[h] + lax.div(h, coarse) + base for h in cols]

    def inner(cols):
        return [h - p * coarse for h in cols]

    return columns, slots_of, inner


def own_kernel(at_ref, pos_ref, cols_ref, a_ref, p_ref, pd_ref, pn_ref, part_ref, ap_ref):
    g, p = lax.axis_index("cols"), lax.axis_index("rows")
    groups = lax.axis_size("cols")
    coarse = groups
    count = a_ref.shape[0]
    fine = p_ref.shape[0]
    start = p * fine + g * count
    edge = edge_of(g, p)
    low = g == 0
    columns, slots_of, inner = lookups(pos_ref, cols_ref)

    for f in range(-HB, count + HB):
        x = p_ref[jnp.clip(count * g + f, 0, fine - 1)]
        if f == -HB:
            x = jnp.where(jnp.logical_and(edge, low), jnp.zeros_like(x), x)
        if f == count + HB - 1:
            x = jnp.where(jnp.logical_and(edge, g > 0), jnp.zeros_like(x), x)
        pairs = turned_pairs(x)
        cols = columns(f)
        spread(pairs, slots_of(cols), groups, pd_ref, f + HB)
        if 0 <= f < count:
            spread(pairs, inner(cols), coarse // 2, pn_ref, f)

    zeros = jnp.where(low, 0, count + 2 * HB - 1)
    first = jnp.where(edge, jnp.where(low, 0, count - HB), count)
    for i in range(count):
        later = jnp.logical_and(i >= first, i < first + HB)
        picks = [at_ref[k, g * count + i] - (start - HB) for k in range(KA)]
        picks = [jnp.where(later, zeros, pick) for pick in picks]
        ap_ref[i * B : (i + 1) * B, :] = ap_row(a_ref[i], picks, pd_ref)
    part_ref[...] = transposed_dot(pn_ref[...], ap_ref[...])


def edge_kernel(
    at_ref, pos_ref, cols_ref, steps_ref, own_a_ref, far_a_ref, far_p_ref, pd_ref, pn_ref, part_ref,
    sent_ref, table, lhs, ap_ref,
):
    g, p = lax.axis_index("cols"), lax.axis_index("rows")
    groups = lax.axis_size("cols")
    edge = edge_of(g, p)
    low = g == 0
    size = HB * B
    count = pn_ref.shape[0] // B
    fine = at_ref.shape[1]
    columns, slots_of, inner = lookups(pos_ref, cols_ref)

    def store(total):
        for c in range(groups):
            sent_ref[c] = total[:, c * LANES : (c + 1) * LANES].astype(jnp.bfloat16)

    def half(second):
        return pl.ds(pl.multiple_of(jnp.where(second, size, 0), size), size)

    @pl.when(edge)
    def _():
        rows = pl.ds(pl.multiple_of(jnp.where(low, 2 * size, 0), size), 2 * size)
        table[rows, :] = pd_ref[size : 3 * size, :]
        lhs[half(low), :] = pn_ref[pl.ds(pl.multiple_of(jnp.where(low, 0, (count - HB) * B), B), size), :]
        shift = jnp.where(low, 0, 2 * HB)
        for t in range(2 * HB):
            cols = columns(jnp.where(low, t - 2 * HB, count + t))
            spread(turned_pairs(far_p_ref[t]), slots_of(cols), groups, table, shift + t)
        for t in range(HB):
            s = jnp.where(low, HB, 0) + t
            cols = columns(jnp.where(low, t - HB, count + t))
            row = jnp.where(low, t, HB + t)
            spread(turned_pairs(far_p_ref[s]), inner(cols), groups // 2, lhs, row)
        first = g * count + jnp.where(low, 0, count - HB)
        base = p * fine + g * count - jnp.where(low, 2 * HB, 0)
        for t in range(HB):
            a = own_a_ref[t]
            picks = [at_ref[k, first + t] - base for k in range(KA)]
            ap_ref[block(jnp.where(low, HB + t, t)), :] = ap_row(a, picks, table)
        for t in range(HB):
            a = far_a_ref[t]
            lane = jnp.where(low, fine - HB, 0) + t
            picks = [steps_ref[k, lane] + jnp.where(low, t, HB + t) for k in range(KA)]
            ap_ref[block(jnp.where(low, t, HB + t)), :] = ap_row(a, picks, table)
        store(part_ref[...] + transposed_dot(lhs[...], ap_ref[...]))

    @pl.when(jnp.logical_not(edge))
    def _():
        store(part_ref[...])


def on_device(a_vals, a_cols, p_vals, p_cols, colpos):
    groups = lax.axis_size("cols")
    parts = lax.axis_size("rows")
    count = a_vals.shape[0]
    fine = p_vals.shape[0]
    coarse = groups
    g = lax.axis_index("cols")
    p = lax.axis_index("rows")
    last = groups - 1
    wide = groups * LANES
    bf16, f32 = jnp.bfloat16, jnp.float32
    params = pltpu.CompilerParams(vmem_limit_bytes=16 << 20)
    at = a_cols.T

    far_row = jnp.where(g < groups // 2, fine - 2 * HB, 0)
    longer = jnp.pad(p_vals, ((0, 1), (0, 0), (0, 0)))
    msg_p = lax.dynamic_slice_in_dim(longer, far_row, 2 * HB + 1, 0)
    steps = (at - (p * fine - HB + jnp.arange(fine, dtype=jnp.int32))).astype(bf16)
    steps = jnp.pad(steps[None], ((2 * HB, 0), (0, B - KA), (0, KP * B - fine)))
    row = lax.broadcasted_iota(jnp.int32, msg_p.shape, 0)
    msg_p = jnp.where(row < 2 * HB, msg_p, steps)
    pairs = [(q * groups + 1, (q + 1) * groups) for q in range(parts - 1)]
    pairs += [((q + 1) * groups + last - 1, q * groups + last) for q in range(parts - 1)]
    far_p = lax.ppermute(msg_p, ("rows", "cols"), pairs)
    msg_a = pl.pallas_call(
        pack_kernel,
        out_shape=jax.ShapeDtypeStruct((HB,) + a_vals.shape[1:], bf16),
        in_specs=[VMEM, pl.BlockSpec(memory_space=pl.ANY)],
        out_specs=VMEM,
        compiler_params=params,
        name="pack",
    )(a_vals, msg_p)
    pairs = [(q * groups, (q - 1) * groups + last) for q in range(1, parts)]
    pairs += [(target, source) for source, target in pairs]
    far_a = lax.ppermute(msg_a, ("rows", "cols"), pairs)

    pad = 2 * HB
    padded = jnp.pad(p_cols.T, ((0, 0), (pad, pad)))
    near_cols = lax.dynamic_slice_in_dim(padded, p * fine + g * count, count + 2 * pad, 1)
    pd, pn, part = pl.pallas_call(
        own_kernel,
        out_shape=(
            jax.ShapeDtypeStruct(((count + 2 * HB) * B, wide), bf16),
            jax.ShapeDtypeStruct((count * B, coarse * B), bf16),
            jax.ShapeDtypeStruct((coarse * B, wide), f32),
        ),
        in_specs=[SMEM] * 3 + [VMEM] * 2,
        out_specs=(VMEM, VMEM, VMEM),
        scratch_shapes=[pltpu.VMEM((count * B, wide), bf16)],
        compiler_params=params,
        cost_estimate=pl.CostEstimate(flops=1 << 31, bytes_accessed=4 << 20, transcendentals=0),
        name="own_rows",
    )(at, colpos, near_cols, a_vals, p_vals)

    far_steps = far_p[2 * HB, :KA, :fine].astype(jnp.int32)
    sent = pl.pallas_call(
        edge_kernel,
        out_shape=jax.ShapeDtypeStruct((groups, coarse * B, LANES), bf16),
        in_specs=[SMEM] * 4 + [VMEM] * 6,
        out_specs=VMEM,
        scratch_shapes=[
            pltpu.VMEM((4 * HB * B, wide), bf16),
            pltpu.VMEM((2 * HB * B, coarse * B), bf16),
            pltpu.VMEM((2 * HB * B, wide), bf16),
        ],
        compiler_params=params,
        name="edge_rows",
    )(at, colpos, near_cols, far_steps, msg_a, far_a, far_p, pd, pn, part)

    got = lax.all_to_all(sent, "cols", 0, 0).astype(f32)
    half = groups // 2
    low = sum(got[c] for c in range(1, half)) + got[0]
    high = sum(got[c] for c in range(half + 1, groups)) + got[half]
    out = jnp.pad(low, ((0, 0), (0, B))) + jnp.pad(high, ((0, 0), (B, 0)))
    return out.reshape(coarse, B, 3 * B)


def solution(mesh):
    placed = (P(("rows", "cols"), None, None), P("rows", None), P("rows", None, None), P(), P())
    return jax.shard_map(
        on_device, mesh=mesh, in_specs=placed, out_specs=P("rows", None, "cols"), check_vma=False
    )
```

time: 29.9 us -> 29.2 us (0.977)
  the two profiles are of different devices: /device:TPU:8 before, /device:TPU:928 now
where the time goes in v4:
time: 29.2 us; the launch traced here: 29 us
  blocking collectives  10.5 us (36%)
  starting transfers between devices  8.3 us (28%)
  Pallas kernels  4.83 us (17%)
  other arithmetic  2.83 us (10%)
  waiting for transfers between devices  2.31 us (8%)
    all_to_all x1, blocking collectives, on_device(): got = lax.all_to_all(sent, 'cols', 0, 0).astype(f32)  10.5 us
    ppermute x1, starting transfers between devices, on_device(): far_a = lax.ppermute(msg_a, ('rows', 'cols'), pairs)  7.01 us
    pallas_call x1, Pallas kernels, on_device(): pl.pallas_call(own_kernel, out_shape=(jax.ShapeDtypeStruct(((count + 2 *...  2.56 us
    pallas_call x1, Pallas kernels, on_device(): pl.pallas_call(edge_kernel, out_shape=jax.ShapeDtypeStruct((groups, coars...  2.24 us
    ppermute x1, waiting for transfers between devices, on_device(): far_a = lax.ppermute(msg_a, ('rows', 'cols'), pairs)  2.2 us
    ppermute x1, starting transfers between devices, on_device(): far_p = lax.ppermute(msg_p, ('rows', 'cols'), pairs)  1.29 us
    select_n x1, other arithmetic, on_device(): msg_p = jnp.where(row < 2 * HB, msg_p, steps)  1.17 us
    add x1, other arithmetic, on_device(): out = jnp.pad(low, ((0, 0), (0, B))) + jnp.pad(high, ((0, 0), (B, 0)))  0.84 us
  transfers between devices with their start and end apart: 2, of which 2 were waited for; matrix products, arithmetic and copies ran while one was open for 0% of the time, Pallas kernels for 9%

profile of v4, /device:TPU:928, one launch (start us, length us, event | category | flops | bytes accessed | tf_op | source)
XLA Modules:
  0.0 29.0 jit_solution(3459001994294859736)
XLA Ops:
  0.0 0.0 copy-start.1
  0.0 0.7 %fusion.3 = bf16[1,8,32]{2,1,0:T(8,128)(2,1)S(1)} fusion(s32[32]{0:T(128)S(1)} %iota_add_fusion, s32[32,8]{0,1:T(8,128)} %param.6), kind=kLoop, calls=%fused_computation.9 | loop fusion | flops 512 | bytes 1664 | tf_op jit(solution)/shard_map/broadcast_in_dim | solution.py:179
  0.8 0.0 copy-start.4
  0.8 0.0 copy-start
  0.8 0.0 copy-start.2
  0.8 0.0 copy-start.3
  0.8 1.2 %fusion._ = bf16[9,64,256]{2,1,0:T(8,128)(2,1)S(1)} fusion(s32[]{:T(128)S(6)} %select_n.13, bf16[32,64,256]{2,1,0:T(8,128)(2,1)} %p_ref.1, bf16[1,8,32]{2,1,0:T(8,128)(2,1)S(1)} %fusion.3, pred[9]{0:T(512)(128)(4,1)S(1)} %iota_compare_fusion), kind=kLoop, calls=%fused_computation.1 | loop fusion | flops 147456 | bytes 1344013 | tf_op jit(solution)/shard_map/jit(_where)/select_n | solution.py:181
  2.0 1.3 %collective-permute-start = (bf16[9,64,256]{2,1,0:T(8,128)(2,1)S(1)}, bf16[9,64,256]{2,1,0:T(8,128)(2,1)S(1)}, u32[]{:S(2)}, u32[]{:S(2)}) collective-permute-start(bf16[9,64,256]{2,1,0:T(8,128)(2,1)S(1)} %fusion._), channel_id=1, source_target_pairs={{1,4},{5,8},{9,12},{13,16},{17,20},{21,24},{25,28},{29,32},{33,36}... | collective-permute-start | bytes 884744 | tf_op jit(solution)/shard_map/ppermute | solution.py:184
  3.3 0.0 copy-done.1
  3.3 7.0 %collective-permute-start.1 = (bf16[4,64,512]{2,1,0:T(8,128)(2,1)S(1)}, bf16[4,64,512]{2,1,0:T(8,128)(2,1)S(1)}, u32[]{:S(2)}, u32[]{:S(2)}) collective-permute-start(bf16[4,64,512]{2,1,0:T(8,128)(2,1)S(1)} %pack.1.own_a_ref), channel_id=1, source_target_pairs={{4,3},{8,7},{12,11},{16,15},{20,19},{24,23},{28,27},{32,31},{36,35... | collective-permute-start | bytes 786440 | tf_op jit(solution)/shard_map/ppermute | solution.py:195
  10.3 0.0 copy-done.4
  10.4 0.1 pad_dynamic-slice_fusion.1.cols_ref
  10.4 0.0 copy-done
  10.4 0.0 copy-done.2
  10.4 0.0 copy-done.3
  10.4 2.6 %own_rows.1 = (bf16[1024,512]{1,0:T(8,128)(2,1)S(1)}, bf16[512,256]{1,0:T(8,128)(2,1)S(1)}, f32[256,512]{1,0:T(8,128)S(1)}) custom-call(s32[8,32]{1,0:T(8,128)S(1)} %bitcast.15, s32[1024]{0:T(1024)S(1)} %copy-done.3, s32[4,24]{1,0:T(4,128)S(1)} %pad_dynamic-slice_fusion.1.cols_ref, bf16[8,64,512]{2,1,0:T(8,128)(2,1)S(1)} %copy-done.1, ...), custom_call_target="tpu_custom_call" | custom-call | flops 2147483648 | bytes 4194304 | tf_op jit(solution)/shard_map/own_rows/pallas_call | solution.py:200
  13.0 0.1 collective-permute-done.far_p_ref
  13.1 2.2 %collective-permute-done.1.far_a_ref = bf16[4,64,512]{2,1,0:T(8,128)(2,1)S(1)} collective-permute-done((bf16[4,64,512]{2,1,0:T(8,128)(2,1)S(1)}, bf16[4,64,512]{2,1,0:T(8,128)(2,1)S(1)}, u32[]{:S(2)}, u32[]{:S(2)}) %collective-permute-start.1) | collective-permute-done | bytes 262176 | tf_op jit(solution)/shard_map/ppermute | solution.py:195
  15.3 2.2 %edge_rows.1 = bf16[4,256,128]{2,1,0:T(8,128)(2,1)S(1)} custom-call(s32[8,32]{1,0:T(8,128)S(1)} %bitcast.16, s32[1024]{0:T(1024)S(1)} %copy-done.3, s32[4,24]{1,0:T(4,128)S(1)} %pad_dynamic-slice_fusion.1.cols_ref, s32[8,32]{1,0:T(8,128)S(1)} %fusion.4.steps_ref, bf16[4,64,512]{2,1,0:T(8,128)(2,1)S(1)} %pack.1.own_a_ref, ...), custom_call_target="tpu_custom_call" | custom-call | tf_op jit(solution)/shard_map/edge_rows/pallas_call | solution.py:216
  17.6 10.5 %all_to_all.5 = bf16[4,256,128]{2,1,0:T(8,128)(2,1)S(1)} all-to-all(bf16[4,256,128]{2,1,0:T(8,128)(2,1)S(1)} %edge_rows.1), channel_id=1, replica_groups=mesh['rows'=256,'cols'=4] {'cols'}, dimensions={0} | all-to-all | bytes 524288 | tf_op jit(solution)/shard_map/all_to_all | solution.py:230
  28.1 0.8 %pad_add_fusion = f32[256,192]{1,0:T(8,128)} fusion(f32[256,128]{1,0:T(8,128)S(1)} %get-tuple-element.12, f32[256,128]{1,0:T(8,128)S(1)} %get-tuple-element.11), kind=kLoop, calls=%fused_computation.2 | loop fusion | flops 49152 | bytes 458752 | tf_op jit(solution)/shard_map/add | solution.py:234
  (6 shorter events, 0.1 us)
Async XLA Ops:
  0.0 3.3 %copy-start.1 = (bf16[8,64,512]{2,1,0:T(8,128)(2,1)S(1)}, bf16[8,64,512]{2,1,0:T(8,128)(2,1)}, u32[]{:S(2)}) copy-start(bf16[8,64,512]{2,1,0:T(8,128)(2,1)} %a_ref.3) | copy-start | bytes 1572868
  0.8 9.6 %copy-start.4 = (s32[8192,4]{0,1:T(4,128)S(1)}, s32[8192,4]{0,1:T(4,128)}, u32[]{:S(2)}) copy-start(s32[8192,4]{0,1:T(4,128)} %param.8) | copy-start | bytes 393220
  0.8 9.7 %copy-start = (bf16[32,64,256]{2,1,0:T(8,128)(2,1)S(1)}, bf16[32,64,256]{2,1,0:T(8,128)(2,1)}, u32[]{:S(2)}) copy-start(bf16[32,64,256]{2,1,0:T(8,128)(2,1)} %p_ref.1) | copy-start | bytes 3145732
  0.8 9.7 %copy-start.2 = (s32[32,8]{0,1:T(8,128)S(1)}, s32[32,8]{0,1:T(8,128)}, u32[]{:S(2)}) copy-start(s32[32,8]{0,1:T(8,128)} %param.6) | copy-start | bytes 3076
  0.8 9.7 %copy-start.3 = (s32[1024]{0:T(1024)S(1)}, s32[1024]{0:T(1024)}, u32[]{:S(2)}) copy-start(s32[1024]{0:T(1024)} %pos_ref.3) | copy-start | bytes 12292
  2.0 11.2 %collective-permute-start = (bf16[9,64,256]{2,1,0:T(8,128)(2,1)S(1)}, bf16[9,64,256]{2,1,0:T(8,128)(2,1)S(1)}, u32[]{:S(2)}, u32[]{:S(2)}) collective-permute-start(bf16[9,64,256]{2,1,0:T(8,128)(2,1)S(1)} %fusion._), channel_id=1, source_target_pairs={{1,4},{5,8},{9,12},{13,16},{17,20},{21,24},{25,28},{29,32},{33,36}... | collective-permute-start | bytes 884744 | tf_op jit(solution)/shard_map/ppermute | solution.py:184
  3.3 12.0 %collective-permute-start.1 = (bf16[4,64,512]{2,1,0:T(8,128)(2,1)S(1)}, bf16[4,64,512]{2,1,0:T(8,128)(2,1)S(1)}, u32[]{:S(2)}, u32[]{:S(2)}) collective-permute-start(bf16[4,64,512]{2,1,0:T(8,128)(2,1)S(1)} %pack.1.own_a_ref), channel_id=1, source_target_pairs={{4,3},{8,7},{12,11},{16,15},{20,19},{24,23},{28,27},{32,31},{36,35... | collective-permute-start | bytes 786440 | tf_op jit(solution)/shard_map/ppermute | solution.py:195

commit v5 on v4

--- a/solution.py
+++ b/solution.py
@@ -106,52 +106,56 @@
     part_ref[...] = transposed_dot(pn_ref[...], ap_ref[...])
 
 
-def edge_kernel(
-    at_ref, pos_ref, cols_ref, steps_ref, own_a_ref, far_a_ref, far_p_ref, pd_ref, pn_ref, part_ref,
-    sent_ref, table, lhs, ap_ref,
+def halo_kernel(
+    at_ref, pos_ref, cols_ref, own_a_ref, far_p_ref, pd_ref, pn_ref, table, lhs, more_ref, ap_ref
 ):
     g, p = lax.axis_index("cols"), lax.axis_index("rows")
     groups = lax.axis_size("cols")
-    edge = edge_of(g, p)
     low = g == 0
     size = HB * B
     count = pn_ref.shape[0] // B
     fine = at_ref.shape[1]
     columns, slots_of, inner = lookups(pos_ref, cols_ref)
 
-    def store(total):
-        for c in range(groups):
-            sent_ref[c] = total[:, c * LANES : (c + 1) * LANES].astype(jnp.bfloat16)
-
-    def half(second):
-        return pl.ds(pl.multiple_of(jnp.where(second, size, 0), size), size)
-
-    @pl.when(edge)
+    @pl.when(edge_of(g, p))
     def _():
         rows = pl.ds(pl.multiple_of(jnp.where(low, 2 * size, 0), size), 2 * size)
         table[rows, :] = pd_ref[size : 3 * size, :]
-        lhs[half(low), :] = pn_ref[pl.ds(pl.multiple_of(jnp.where(low, 0, (count - HB) * B), B), size), :]
         shift = jnp.where(low, 0, 2 * HB)
         for t in range(2 * HB):
             cols = columns(jnp.where(low, t - 2 * HB, count + t))
             spread(turned_pairs(far_p_ref[t]), slots_of(cols), groups, table, shift + t)
         for t in range(HB):
-            s = jnp.where(low, HB, 0) + t
             cols = columns(jnp.where(low, t - HB, count + t))
-            row = jnp.where(low, t, HB + t)
-            spread(turned_pairs(far_p_ref[s]), inner(cols), groups // 2, lhs, row)
-        first = g * count + jnp.where(low, 0, count - HB)
+            row = turned_pairs(far_p_ref[jnp.where(low, HB, 0) + t])
+            spread(row, inner(cols), groups // 2, lhs, t)
+        first = jnp.where(low, 0, count - HB)
         base = p * fine + g * count - jnp.where(low, 2 * HB, 0)
         for t in range(HB):
-            a = own_a_ref[t]
-            picks = [at_ref[k, first + t] - base for k in range(KA)]
-            ap_ref[block(jnp.where(low, HB + t, t)), :] = ap_row(a, picks, table)
+            picks = [at_ref[k, g * count + first + t] - base for k in range(KA)]
+            ap_ref[t * B : (t + 1) * B, :] = ap_row(own_a_ref[t], picks, table)
+        own = pn_ref[pl.ds(pl.multiple_of(first * B, B), size), :]
+        more_ref[...] = transposed_dot(own, ap_ref[...])
+
+
+def edge_kernel(steps_ref, far_a_ref, table, lhs, part_ref, more_ref, sent_ref, ap_ref):
+    g, p = lax.axis_index("cols"), lax.axis_index("rows")
+    groups = lax.axis_size("cols")
+    edge = edge_of(g, p)
+    low = g == 0
+    fine = steps_ref.shape[1]
+
+    def store(total):
+        for c in range(groups):
+            sent_ref[c] = total[:, c * LANES : (c + 1) * LANES].astype(jnp.bfloat16)
+
+    @pl.when(edge)
+    def _():
         for t in range(HB):
-            a = far_a_ref[t]
             lane = jnp.where(low, fine - HB, 0) + t
             picks = [steps_ref[k, lane] + jnp.where(low, t, HB + t) for k in range(KA)]
-            ap_ref[block(jnp.where(low, t, HB + t)), :] = ap_row(a, picks, table)
-        store(part_ref[...] + transposed_dot(lhs[...], ap_ref[...]))
+            ap_ref[t * B : (t + 1) * B, :] = ap_row(far_a_ref[t], picks, table)
+        store(part_ref[...] + more_ref[...] + transposed_dot(lhs[...], ap_ref[...]))
 
     @pl.when(jnp.logical_not(edge))
     def _():
@@ -212,20 +216,31 @@
         name="own_rows",
     )(at, colpos, near_cols, a_vals, p_vals)
 
+    table, far_pn, more = pl.pallas_call(
+        halo_kernel,
+        out_shape=(
+            jax.ShapeDtypeStruct((4 * HB * B, wide), bf16),
+            jax.ShapeDtypeStruct((HB * B, coarse * B), bf16),
+            jax.ShapeDtypeStruct((coarse * B, wide), f32),
+        ),
+        in_specs=[SMEM] * 3 + [VMEM] * 4,
+        out_specs=(VMEM, VMEM, VMEM),
+        scratch_shapes=[pltpu.VMEM((HB * B, wide), bf16)],
+        compiler_params=params,
+        cost_estimate=pl.CostEstimate(flops=1 << 30, bytes_accessed=2 << 20, transcendentals=0),
+        name="halo_rows",
+    )(at, colpos, near_cols, msg_a, far_p, pd, pn)
+
     far_steps = far_p[2 * HB, :KA, :fine].astype(jnp.int32)
     sent = pl.pallas_call(
         edge_kernel,
         out_shape=jax.ShapeDtypeStruct((groups, coarse * B, LANES), bf16),
-        in_specs=[SMEM] * 4 + [VMEM] * 6,
+        in_specs=[SMEM] + [VMEM] * 5,
         out_specs=VMEM,
-        scratch_shapes=[
-            pltpu.VMEM((4 * HB * B, wide), bf16),
-            pltpu.VMEM((2 * HB * B, coarse * B), bf16),
-            pltpu.VMEM((2 * HB * B, wide), bf16),
-        ],
+        scratch_shapes=[pltpu.VMEM((HB * B, wide), bf16)],
         compiler_params=params,
         name="edge_rows",
-    )(at, colpos, near_cols, far_steps, msg_a, far_a, far_p, pd, pn, part)
+    )(far_steps, far_a, table, far_pn, part, more)
 
     got = lax.all_to_all(sent, "cols", 0, 0).astype(f32)
     half = groups // 2

time: 29.2 us -> 29.3 us (level)
  the two profiles are of different devices: /device:TPU:928 before, /device:TPU:8 now
where the time goes in v5:
time: 29.3 us; the launch traced here: 29.1 us
  blocking collectives  19.3 us (66%)
  Pallas kernels  3.96 us (14%)
  other arithmetic  2.83 us (10%)
  starting transfers between devices  1.99 us (7%)
  waiting for transfers between devices  0.8 us (3%)
    all_to_all x1, blocking collectives, on_device(): got = lax.all_to_all(sent, 'cols', 0, 0).astype(f32)  19.3 us
    pallas_call x1, Pallas kernels, on_device(): pl.pallas_call(own_kernel, out_shape=(jax.ShapeDtypeStruct(((count + 2 *...  2.56 us
    ppermute x1, starting transfers between devices, on_device(): far_p = lax.ppermute(msg_p, ('rows', 'cols'), pairs)  1.31 us
    select_n x1, other arithmetic, on_device(): msg_p = jnp.where(row < 2 * HB, msg_p, steps)  1.17 us
    add x1, other arithmetic, on_device(): out = jnp.pad(low, ((0, 0), (0, B))) + jnp.pad(high, ((0, 0), (B, 0)))  0.84 us
    ppermute x1, waiting for transfers between devices, on_device(): far_p = lax.ppermute(msg_p, ('rows', 'cols'), pairs)  0.79 us
    broadcast_in_dim x1, other arithmetic, on_device(): steps = jnp.pad(steps[None], ((2 * HB, 0), (0, B - KA), (0, KP * B - fine)))  0.75 us
    pallas_call x1, Pallas kernels, on_device(): pl.pallas_call(halo_kernel, out_shape=(jax.ShapeDtypeStruct((4 * HB * B,...  0.71 us
  transfers between devices with their start and end apart: 2, of which 1 were waited for; matrix products, arithmetic and copies ran while one was open for 0% of the time, Pallas kernels for 11%

profile of v5, /device:TPU:8, one launch (start us, length us, event | category | flops | bytes accessed | tf_op | source)
XLA Modules:
  0.0 29.1 jit_solution(305253399339442615)
XLA Ops:
  0.0 0.0 copy-start.1
  0.0 0.7 %fusion.3 = bf16[1,8,32]{2,1,0:T(8,128)(2,1)S(1)} fusion(s32[32]{0:T(128)S(1)} %iota_add_fusion, s32[32,8]{0,1:T(8,128)} %param.6), kind=kLoop, calls=%fused_computation.9 | loop fusion | flops 512 | bytes 1664 | tf_op jit(solution)/shard_map/broadcast_in_dim | solution.py:183
  0.8 0.0 copy-start.4
  0.8 0.0 copy-start
  0.8 0.0 copy-start.2
  0.8 0.0 copy-start.3
  0.8 1.2 %fusion._ = bf16[9,64,256]{2,1,0:T(8,128)(2,1)S(1)} fusion(s32[]{:T(128)S(6)} %select_n.12, bf16[32,64,256]{2,1,0:T(8,128)(2,1)} %p_ref.1, bf16[1,8,32]{2,1,0:T(8,128)(2,1)S(1)} %fusion.3, pred[9]{0:T(512)(128)(4,1)S(1)} %iota_compare_fusion), kind=kLoop, calls=%fused_computation.1 | loop fusion | flops 147456 | bytes 1344013 | tf_op jit(solution)/shard_map/jit(_where)/select_n | solution.py:185
  2.0 1.3 %collective-permute-start = (bf16[9,64,256]{2,1,0:T(8,128)(2,1)S(1)}, bf16[9,64,256]{2,1,0:T(8,128)(2,1)S(1)}, u32[]{:S(2)}, u32[]{:S(2)}) collective-permute-start(bf16[9,64,256]{2,1,0:T(8,128)(2,1)S(1)} %fusion._), channel_id=1, source_target_pairs={{1,4},{5,8},{9,12},{13,16},{17,20},{21,24},{25,28},{29,32},{33,36}... | collective-permute-start | bytes 884744 | tf_op jit(solution)/shard_map/ppermute | solution.py:188
  3.3 0.0 copy-done.1
  3.3 0.7 %collective-permute-start.1 = (bf16[4,64,512]{2,1,0:T(8,128)(2,1)S(1)}, bf16[4,64,512]{2,1,0:T(8,128)(2,1)S(1)}, u32[]{:S(2)}, u32[]{:S(2)}) collective-permute-start(bf16[4,64,512]{2,1,0:T(8,128)(2,1)S(1)} %pack.1.own_a_ref), channel_id=1, source_target_pairs={{4,3},{8,7},{12,11},{16,15},{20,19},{24,23},{28,27},{32,31},{36,35... | collective-permute-start | bytes 786440 | tf_op jit(solution)/shard_map/ppermute | solution.py:199
  4.0 0.0 copy-done.4
  4.0 0.1 pad_dynamic-slice_fusion.1.cols_ref
  4.1 0.0 copy-done
  4.1 0.0 copy-done.2
  4.1 0.0 copy-done.3
  4.1 2.6 %own_rows.1 = (bf16[1024,512]{1,0:T(8,128)(2,1)S(1)}, bf16[512,256]{1,0:T(8,128)(2,1)S(1)}, f32[256,512]{1,0:T(8,128)S(1)}) custom-call(s32[8,32]{1,0:T(8,128)S(1)} %bitcast.15, s32[1024]{0:T(1024)S(1)} %copy-done.3, s32[4,24]{1,0:T(4,128)S(1)} %pad_dynamic-slice_fusion.1.cols_ref, bf16[8,64,512]{2,1,0:T(8,128)(2,1)S(1)} %copy-done.1, ...), custom_call_target="tpu_custom_call" | custom-call | flops 2147483648 | bytes 4194304 | tf_op jit(solution)/shard_map/own_rows/pallas_call | solution.py:204
  6.7 0.8 %collective-permute-done.far_p_ref = bf16[9,64,256]{2,1,0:T(8,128)(2,1)S(1)} collective-permute-done((bf16[9,64,256]{2,1,0:T(8,128)(2,1)S(1)}, bf16[9,64,256]{2,1,0:T(8,128)(2,1)S(1)}, u32[]{:S(2)}, u32[]{:S(2)}) %collective-permute-start) | collective-permute-done | bytes 294944 | tf_op jit(solution)/shard_map/ppermute | solution.py:188
  7.5 0.7 %halo_rows.1 = (bf16[1024,512]{1,0:T(8,128)(2,1)S(1)}, bf16[256,256]{1,0:T(8,128)(2,1)S(1)}, f32[256,512]{1,0:T(8,128)S(1)}) custom-call(s32[8,32]{1,0:T(8,128)S(1)} %bitcast.16, s32[1024]{0:T(1024)S(1)} %copy-done.3, s32[4,24]{1,0:T(4,128)S(1)} %pad_dynamic-slice_fusion.1.cols_ref, bf16[4,64,512]{2,1,0:T(8,128)(2,1)S(1)} %pack.1.own_a_ref, ...), custom_call_target="tpu_custom_call" | custom-call | flops 1073741824 | bytes 2097152 | tf_op jit(solution)/shard_map/halo_rows/pallas_call | solution.py:219
  8.2 0.0 collective-permute-done.1.far_a_ref
  8.2 0.7 %edge_rows.1 = bf16[4,256,128]{2,1,0:T(8,128)(2,1)S(1)} custom-call(s32[8,32]{1,0:T(8,128)S(1)} %fusion.4.steps_ref, bf16[4,64,512]{2,1,0:T(8,128)(2,1)S(1)} %collective-permute-done.1.far_a_ref, bf16[1024,512]{1,0:T(8,128)(2,1)S(1)} %get-tuple-element.13.table, bf16[256,256]{1,0:T(8,128)(2,1)S(1)} %get-tuple-element.14.lhs, ...), custom_call_target="tpu_custom_call" | custom-call | tf_op jit(solution)/shard_map/edge_rows/pallas_call | solution.py:235
  8.9 19.3 %all_to_all.5 = bf16[4,256,128]{2,1,0:T(8,128)(2,1)S(1)} all-to-all(bf16[4,256,128]{2,1,0:T(8,128)(2,1)S(1)} %edge_rows.1), channel_id=1, replica_groups=mesh['rows'=256,'cols'=4] {'cols'}, dimensions={0} | all-to-all | bytes 524288 | tf_op jit(solution)/shard_map/all_to_all | solution.py:245
  28.3 0.8 %pad_add_fusion = f32[256,192]{1,0:T(8,128)} fusion(f32[256,128]{1,0:T(8,128)S(1)} %get-tuple-element.18, f32[256,128]{1,0:T(8,128)S(1)} %get-tuple-element.17), kind=kLoop, calls=%fused_computation.2 | loop fusion | flops 49152 | bytes 458752 | tf_op jit(solution)/shard_map/add | solution.py:249
  (6 shorter events, 0.1 us)
Async XLA Ops:
  0.0 3.3 %copy-start.1 = (bf16[8,64,512]{2,1,0:T(8,128)(2,1)S(1)}, bf16[8,64,512]{2,1,0:T(8,128)(2,1)}, u32[]{:S(2)}) copy-start(bf16[8,64,512]{2,1,0:T(8,128)(2,1)} %a_ref.3) | copy-start | bytes 1572868
  0.8 3.2 %copy-start.4 = (s32[8192,4]{0,1:T(4,128)S(1)}, s32[8192,4]{0,1:T(4,128)}, u32[]{:S(2)}) copy-start(s32[8192,4]{0,1:T(4,128)} %param.8) | copy-start | bytes 393220
  0.8 3.3 %copy-start = (bf16[32,64,256]{2,1,0:T(8,128)(2,1)S(1)}, bf16[32,64,256]{2,1,0:T(8,128)(2,1)}, u32[]{:S(2)}) copy-start(bf16[32,64,256]{2,1,0:T(8,128)(2,1)} %p_ref.1) | copy-start | bytes 3145732
  0.8 3.3 %copy-start.2 = (s32[32,8]{0,1:T(8,128)S(1)}, s32[32,8]{0,1:T(8,128)}, u32[]{:S(2)}) copy-start(s32[32,8]{0,1:T(8,128)} %param.6) | copy-start | bytes 3076
  0.8 3.3 %copy-start.3 = (s32[1024]{0:T(1024)S(1)}, s32[1024]{0:T(1024)}, u32[]{:S(2)}) copy-start(s32[1024]{0:T(1024)} %pos_ref.3) | copy-start | bytes 12292
  2.0 5.5 %collective-permute-start = (bf16[9,64,256]{2,1,0:T(8,128)(2,1)S(1)}, bf16[9,64,256]{2,1,0:T(8,128)(2,1)S(1)}, u32[]{:S(2)}, u32[]{:S(2)}) collective-permute-start(bf16[9,64,256]{2,1,0:T(8,128)(2,1)S(1)} %fusion._), channel_id=1, source_target_pairs={{1,4},{5,8},{9,12},{13,16},{17,20},{21,24},{25,28},{29,32},{33,36}... | collective-permute-start | bytes 884744 | tf_op jit(solution)/shard_map/ppermute | solution.py:188
  3.3 4.9 %collective-permute-start.1 = (bf16[4,64,512]{2,1,0:T(8,128)(2,1)S(1)}, bf16[4,64,512]{2,1,0:T(8,128)(2,1)S(1)}, u32[]{:S(2)}, u32[]{:S(2)}) collective-permute-start(bf16[4,64,512]{2,1,0:T(8,128)(2,1)S(1)} %pack.1.own_a_ref), channel_id=1, source_target_pairs={{4,3},{8,7},{12,11},{16,15},{20,19},{24,23},{28,27},{32,31},{36,35... | collective-permute-start | bytes 786440 | tf_op jit(solution)/shard_map/ppermute | solution.py:199

commit v6 on v5

--- a/solution.py
+++ b/solution.py
@@ -12,6 +12,7 @@
 LANES = 2 * B
 VMEM = pl.BlockSpec(memory_space=pltpu.VMEM)
 SMEM = pl.BlockSpec(memory_space=pltpu.SMEM)
+ANY = pl.BlockSpec(memory_space=pl.ANY)
 
 
 def block(i):
@@ -107,7 +108,9 @@
 
 
 def halo_kernel(
-    at_ref, pos_ref, cols_ref, own_a_ref, far_p_ref, pd_ref, pn_ref, table, lhs, more_ref, ap_ref
+    at_hbm, pos_hbm, cols_hbm, own_a_ref, far_p_ref, pd_ref, pn_ref,
+    table, lhs, more_ref,
+    ap_ref, at_ref, pos_ref, cols_ref, sems,
 ):
     g, p = lax.axis_index("cols"), lax.axis_index("rows")
     groups = lax.axis_size("cols")
@@ -119,8 +122,14 @@
 
     @pl.when(edge_of(g, p))
     def _():
+        pairs = [(at_hbm, at_ref), (pos_hbm, pos_ref), (cols_hbm, cols_ref)]
+        copies = [pltpu.make_async_copy(x, y, sems.at[n]) for n, (x, y) in enumerate(pairs)]
+        for copy in copies:
+            copy.start()
         rows = pl.ds(pl.multiple_of(jnp.where(low, 2 * size, 0), size), 2 * size)
         table[rows, :] = pd_ref[size : 3 * size, :]
+        for copy in copies:
+            copy.wait()
         shift = jnp.where(low, 0, 2 * HB)
         for t in range(2 * HB):
             cols = columns(jnp.where(low, t - 2 * HB, count + t))
@@ -138,7 +147,9 @@
         more_ref[...] = transposed_dot(own, ap_ref[...])
 
 
-def edge_kernel(steps_ref, far_a_ref, table, lhs, part_ref, more_ref, sent_ref, ap_ref):
+def edge_kernel(
+    steps_hbm, far_a_ref, table, lhs, part_ref, more_ref, sent_ref, ap_ref, steps_ref, sem
+):
     g, p = lax.axis_index("cols"), lax.axis_index("rows")
     groups = lax.axis_size("cols")
     edge = edge_of(g, p)
@@ -151,6 +162,9 @@
 
     @pl.when(edge)
     def _():
+        copy = pltpu.make_async_copy(steps_hbm, steps_ref, sem)
+        copy.start()
+        copy.wait()
         for t in range(HB):
             lane = jnp.where(low, fine - HB, 0) + t
             picks = [steps_ref[k, lane] + jnp.where(low, t, HB + t) for k in range(KA)]
@@ -223,9 +237,15 @@
             jax.ShapeDtypeStruct((HB * B, coarse * B), bf16),
             jax.ShapeDtypeStruct((coarse * B, wide), f32),
         ),
-        in_specs=[SMEM] * 3 + [VMEM] * 4,
+        in_specs=[ANY] * 3 + [VMEM] * 4,
         out_specs=(VMEM, VMEM, VMEM),
-        scratch_shapes=[pltpu.VMEM((HB * B, wide), bf16)],
+        scratch_shapes=[
+            pltpu.VMEM((HB * B, wide), bf16),
+            pltpu.SMEM(at.shape, jnp.int32),
+            pltpu.SMEM(colpos.shape, jnp.int32),
+            pltpu.SMEM(near_cols.shape, jnp.int32),
+            pltpu.SemaphoreType.DMA((3,)),
+        ],
         compiler_params=params,
         cost_estimate=pl.CostEstimate(flops=1 << 30, bytes_accessed=2 << 20, transcendentals=0),
         name="halo_rows",
@@ -235,9 +255,13 @@
     sent = pl.pallas_call(
         edge_kernel,
         out_shape=jax.ShapeDtypeStruct((groups, coarse * B, LANES), bf16),
-        in_specs=[SMEM] + [VMEM] * 5,
+        in_specs=[ANY] + [VMEM] * 5,
         out_specs=VMEM,
-        scratch_shapes=[pltpu.VMEM((HB * B, wide), bf16)],
+        scratch_shapes=[
+            pltpu.VMEM((HB * B, wide), bf16),
+            pltpu.SMEM(at.shape, jnp.int32),
+            pltpu.SemaphoreType.DMA,
+        ],
         compiler_params=params,
         name="edge_rows",
     )(far_steps, far_a, table, far_pn, part, more)

time: 29.3 us -> 28.4 us (0.969)
  the two profiles are of different devices: /device:TPU:8 before, /device:TPU:966 now
where the time goes in v6:
time: 28.4 us; the launch traced here: 28.2 us
  blocking collectives  12.8 us (45%)
  starting transfers between devices  5.93 us (21%)
  Pallas kernels  5.59 us (20%)
  other arithmetic  2.83 us (10%)
  waiting for transfers between devices  0.86 us (3%)
    all_to_all x1, blocking collectives, on_device(): got = lax.all_to_all(sent, 'cols', 0, 0).astype(f32)  12.8 us
    ppermute x1, starting transfers between devices, on_device(): far_a = lax.ppermute(msg_a, ('rows', 'cols'), pairs)  4.64 us
    pallas_call x1, Pallas kernels, on_device(): pl.pallas_call(own_kernel, out_shape=(jax.ShapeDtypeStruct(((count + 2 *...  2.56 us
    pallas_call x1, Pallas kernels, on_device(): pl.pallas_call(halo_kernel, out_shape=(jax.ShapeDtypeStruct((4 * HB * B,...  1.71 us
    ppermute x1, starting transfers between devices, on_device(): far_p = lax.ppermute(msg_p, ('rows', 'cols'), pairs)  1.29 us
    pallas_call x1, Pallas kernels, on_device(): pl.pallas_call(edge_kernel, out_shape=jax.ShapeDtypeStruct((groups, coars...  1.29 us
    select_n x1, other arithmetic, on_device(): msg_p = jnp.where(row < 2 * HB, msg_p, steps)  1.17 us
    add x1, other arithmetic, on_device(): out = jnp.pad(low, ((0, 0), (0, B))) + jnp.pad(high, ((0, 0), (B, 0)))  0.84 us
  transfers between devices with their start and end apart: 2, of which 2 were waited for; matrix products, arithmetic and copies ran while one was open for 0% of the time, Pallas kernels for 15%

profile of v6, /device:TPU:966, one launch (start us, length us, event | category | flops | bytes accessed | tf_op | source)
XLA Modules:
  0.0 28.2 jit_solution(12621193744689015958)
XLA Ops:
  0.0 0.0 copy-start.1
  0.0 0.7 %fusion.3 = bf16[1,8,32]{2,1,0:T(8,128)(2,1)S(1)} fusion(s32[32]{0:T(128)S(1)} %iota_add_fusion, s32[32,8]{0,1:T(8,128)} %param.6), kind=kLoop, calls=%fused_computation.9 | loop fusion | flops 512 | bytes 1664 | tf_op jit(solution)/shard_map/broadcast_in_dim | solution.py:197
  0.8 0.0 copy-start.4
  0.8 0.0 copy-start
  0.8 0.0 copy-start.2
  0.8 0.0 copy-start.3
  0.8 1.2 %fusion._ = bf16[9,64,256]{2,1,0:T(8,128)(2,1)S(1)} fusion(s32[]{:T(128)S(6)} %select_n.12, bf16[32,64,256]{2,1,0:T(8,128)(2,1)} %p_ref.1, bf16[1,8,32]{2,1,0:T(8,128)(2,1)S(1)} %fusion.3, pred[9]{0:T(512)(128)(4,1)S(1)} %iota_compare_fusion), kind=kLoop, calls=%fused_computation.1 | loop fusion | flops 147456 | bytes 1344013 | tf_op jit(solution)/shard_map/jit(_where)/select_n | solution.py:199
  2.0 1.3 %collective-permute-start = (bf16[9,64,256]{2,1,0:T(8,128)(2,1)S(1)}, bf16[9,64,256]{2,1,0:T(8,128)(2,1)S(1)}, u32[]{:S(2)}, u32[]{:S(2)}) collective-permute-start(bf16[9,64,256]{2,1,0:T(8,128)(2,1)S(1)} %fusion._), channel_id=1, source_target_pairs={{1,4},{5,8},{9,12},{13,16},{17,20},{21,24},{25,28},{29,32},{33,36}... | collective-permute-start | bytes 884744 | tf_op jit(solution)/shard_map/ppermute | solution.py:202
  3.3 0.0 copy-done.1
  3.3 4.6 %collective-permute-start.1 = (bf16[4,64,512]{2,1,0:T(8,128)(2,1)S(1)}, bf16[4,64,512]{2,1,0:T(8,128)(2,1)S(1)}, u32[]{:S(2)}, u32[]{:S(2)}) collective-permute-start(bf16[4,64,512]{2,1,0:T(8,128)(2,1)S(1)} %pack.1.own_a_ref), channel_id=1, source_target_pairs={{4,3},{8,7},{12,11},{16,15},{20,19},{24,23},{28,27},{32,31},{36,35... | collective-permute-start | bytes 786440 | tf_op jit(solution)/shard_map/ppermute | solution.py:213
  8.0 0.0 copy-done.4
  8.0 0.1 pad_dynamic-slice_fusion.1.cols_ref.cols_hbm
  8.1 0.0 copy-done
  8.1 0.0 copy-done.2
  8.1 0.0 copy-done.3
  8.1 2.6 %own_rows.1 = (bf16[1024,512]{1,0:T(8,128)(2,1)S(1)}, bf16[512,256]{1,0:T(8,128)(2,1)S(1)}, f32[256,512]{1,0:T(8,128)S(1)}) custom-call(s32[8,32]{1,0:T(8,128)S(1)} %bitcast.15, s32[1024]{0:T(1024)S(1)} %copy-done.3, s32[4,24]{1,0:T(4,128)S(1)} %pad_dynamic-slice_fusion.1.cols_ref.cols_hbm, bf16[8,64,512]{2,1,0:T(8,128)(2,1)S(1)} %copy-done.1, ...), custom_call_target="tpu_custom_call" | custom-call | flops 2147483648 | bytes 4194304 | tf_op jit(solution)/shard_map/own_rows/pallas_call | solution.py:218
  10.6 0.4 %collective-permute-done.far_p_ref = bf16[9,64,256]{2,1,0:T(8,128)(2,1)S(1)} collective-permute-done((bf16[9,64,256]{2,1,0:T(8,128)(2,1)S(1)}, bf16[9,64,256]{2,1,0:T(8,128)(2,1)S(1)}, u32[]{:S(2)}, u32[]{:S(2)}) %collective-permute-start) | collective-permute-done | bytes 294944 | tf_op jit(solution)/shard_map/ppermute | solution.py:202
  11.0 1.7 %halo_rows.1 = (bf16[1024,512]{1,0:T(8,128)(2,1)S(1)}, bf16[256,256]{1,0:T(8,128)(2,1)S(1)}, f32[256,512]{1,0:T(8,128)S(1)}) custom-call(s32[8,32]{1,0:T(8,128)S(1)} %bitcast.16, s32[1024]{0:T(1024)S(1)} %copy-done.3, s32[4,24]{1,0:T(4,128)S(1)} %pad_dynamic-slice_fusion.1.cols_ref.cols_hbm, bf16[4,64,512]{2,1,0:T(8,128)(2,1)S(1)} %pack.1.own_a_ref, ...), custom_call_target="tpu_custom_call" | custom-call | flops 1073741824 | bytes 2097152 | tf_op jit(solution)/shard_map/halo_rows/pallas_call | solution.py:233
  12.7 0.5 %collective-permute-done.1.far_a_ref = bf16[4,64,512]{2,1,0:T(8,128)(2,1)S(1)} collective-permute-done((bf16[4,64,512]{2,1,0:T(8,128)(2,1)S(1)}, bf16[4,64,512]{2,1,0:T(8,128)(2,1)S(1)}, u32[]{:S(2)}, u32[]{:S(2)}) %collective-permute-start.1) | collective-permute-done | bytes 262176 | tf_op jit(solution)/shard_map/ppermute | solution.py:213
  13.2 1.3 %edge_rows.1 = bf16[4,256,128]{2,1,0:T(8,128)(2,1)S(1)} custom-call(s32[8,32]{1,0:T(8,128)S(1)} %fusion.4.steps_hbm, bf16[4,64,512]{2,1,0:T(8,128)(2,1)S(1)} %collective-permute-done.1.far_a_ref, bf16[1024,512]{1,0:T(8,128)(2,1)S(1)} %get-tuple-element.13.table, bf16[256,256]{1,0:T(8,128)(2,1)S(1)} %get-tuple-element.14.lhs, ...), custom_call_target="tpu_custom_call" | custom-call | tf_op jit(solution)/shard_map/edge_rows/pallas_call | solution.py:255
  14.5 12.8 %all_to_all.5 = bf16[4,256,128]{2,1,0:T(8,128)(2,1)S(1)} all-to-all(bf16[4,256,128]{2,1,0:T(8,128)(2,1)S(1)} %edge_rows.1), channel_id=1, replica_groups=mesh['rows'=256,'cols'=4] {'cols'}, dimensions={0} | all-to-all | bytes 524288 | tf_op jit(solution)/shard_map/all_to_all | solution.py:269
  27.4 0.8 %pad_add_fusion = f32[256,192]{1,0:T(8,128)} fusion(f32[256,128]{1,0:T(8,128)S(1)} %get-tuple-element.18, f32[256,128]{1,0:T(8,128)S(1)} %get-tuple-element.17), kind=kLoop, calls=%fused_computation.2 | loop fusion | flops 49152 | bytes 458752 | tf_op jit(solution)/shard_map/add | solution.py:273
  (6 shorter events, 0.1 us)
Async XLA Ops:
  0.0 3.3 %copy-start.1 = (bf16[8,64,512]{2,1,0:T(8,128)(2,1)S(1)}, bf16[8,64,512]{2,1,0:T(8,128)(2,1)}, u32[]{:S(2)}) copy-start(bf16[8,64,512]{2,1,0:T(8,128)(2,1)} %a_ref.3) | copy-start | bytes 1572868
  0.8 7.2 %copy-start.4 = (s32[8192,4]{0,1:T(4,128)S(1)}, s32[8192,4]{0,1:T(4,128)}, u32[]{:S(2)}) copy-start(s32[8192,4]{0,1:T(4,128)} %param.8) | copy-start | bytes 393220
  0.8 7.3 %copy-start = (bf16[32,64,256]{2,1,0:T(8,128)(2,1)S(1)}, bf16[32,64,256]{2,1,0:T(8,128)(2,1)}, u32[]{:S(2)}) copy-start(bf16[32,64,256]{2,1,0:T(8,128)(2,1)} %p_ref.1) | copy-start | bytes 3145732
  0.8 7.3 %copy-start.2 = (s32[32,8]{0,1:T(8,128)S(1)}, s32[32,8]{0,1:T(8,128)}, u32[]{:S(2)}) copy-start(s32[32,8]{0,1:T(8,128)} %param.6) | copy-start | bytes 3076
  0.8 7.3 %copy-start.3 = (s32[1024]{0:T(1024)S(1)}, s32[1024]{0:T(1024)}, u32[]{:S(2)}) copy-start(s32[1024]{0:T(1024)} %pos_hbm.1) | copy-start | bytes 12292
  2.0 9.0 %collective-permute-start = (bf16[9,64,256]{2,1,0:T(8,128)(2,1)S(1)}, bf16[9,64,256]{2,1,0:T(8,128)(2,1)S(1)}, u32[]{:S(2)}, u32[]{:S(2)}) collective-permute-start(bf16[9,64,256]{2,1,0:T(8,128)(2,1)S(1)} %fusion._), channel_id=1, source_target_pairs={{1,4},{5,8},{9,12},{13,16},{17,20},{21,24},{25,28},{29,32},{33,36}... | collective-permute-start | bytes 884744 | tf_op jit(solution)/shard_map/ppermute | solution.py:202
  3.3 9.9 %collective-permute-start.1 = (bf16[4,64,512]{2,1,0:T(8,128)(2,1)S(1)}, bf16[4,64,512]{2,1,0:T(8,128)(2,1)S(1)}, u32[]{:S(2)}, u32[]{:S(2)}) collective-permute-start(bf16[4,64,512]{2,1,0:T(8,128)(2,1)S(1)} %pack.1.own_a_ref), channel_id=1, source_target_pairs={{4,3},{8,7},{12,11},{16,15},{20,19},{24,23},{28,27},{32,31},{36,35... | collective-permute-start | bytes 786440 | tf_op jit(solution)/shard_map/ppermute | solution.py:213
